TPU v7x, 768 devices: a whole 4x8x12 slice. The times are simulated.
768 devices in a mesh: replica: 8 (over y), fsdp: 96 (over z, x, core).
Axes of the slice: x: 4, y: 8, z: 12, core: 2. Of those that a mesh axis runs over, the one named last changes fastest.
Arguments:
- grad: bfloat16 [72, 672, 672], P(None, 'fsdp', 'replica')
- owner: int32 [72], replicated, may hold values from 0 to 95, as said below
- row_extent: int32 [72], replicated, may hold values from 336 to 672
- col_extent: int32 [72], replicated, may hold values from 336 to 672
- left_old: float32 [96, 672, 672], P('fsdp', 'replica')
- right_old: float32 [96, 672, 672], P('fsdp', 'replica')
- left_root: float32 [96, 672, 672], P('fsdp')
- right_root: float32 [96, 672, 672], P('fsdp', 'replica'), as said below
Outputs:
- update: bfloat16 [72, 672, 672], P(None, 'fsdp', 'replica')
- left_new: float32 [96, 672, 672], P('fsdp', 'replica')
- right_new: float32 [96, 672, 672], P('fsdp', 'replica')
Inputs may be any that keep to these rules, and one draw needn't show every extreme that they name: `owner`: the 72 values are distinct, so that an fsdp index owns at most one block. `right_root`: each of the 96 matrices is symmetric.
All inputs are finite; a program needn't handle non-finite values.
Results may differ from a plain program's by a relative error of at most 0.012.
Values may be sent and summed in bfloat16 or wider, within the bound.
No kernel may reach another device: no remote copies, remote signals or barrier semaphores. Data moves between devices by JAX's collectives and lax.ppermute only.
A program may use at most 32 MiB of HBM per device.

v0:
```python
import jax
import jax.numpy as jnp
from jax import lax
from jax.sharding import PartitionSpec as P

decay_rate = 0.9


def body(grad, owner, row_extent, col_extent, left_old, right_old, left_root, right_root):
    fsdp_count = lax.axis_size("fsdp")
    fsdp_index = lax.axis_index("fsdp")
    replica_index = lax.axis_index("replica")
    row_share = grad.shape[1]
    col_share = grad.shape[2]
    block_order = row_share * fsdp_count
    row_index = fsdp_index * row_share + jnp.arange(row_share, dtype=jnp.int32)
    col_index = replica_index * col_share + jnp.arange(col_share, dtype=jnp.int32)
    live_mask = (row_index[None, :, None] < row_extent[:, None, None]) & (
        col_index[None, None, :] < col_extent[:, None, None]
    )
    masked = jnp.where(live_mask, grad, jnp.zeros_like(grad))
    owners = jnp.arange(fsdp_count, dtype=jnp.int32)
    select = (owner[None, :] == owners[:, None]).astype(jnp.bfloat16)
    outgoing = jnp.einsum("ob,bic->oci", select, masked, preferred_element_type=jnp.float32).astype(
        jnp.bfloat16
    )
    columns = lax.all_to_all(outgoing, "fsdp", split_axis=0, concat_axis=2, tiled=True)[0]
    owned_mask = owner == fsdp_index
    owned_rows = jnp.sum(jnp.where(owned_mask, row_extent, 0))
    owned_cols = jnp.sum(jnp.where(owned_mask, col_extent, 0))
    rows_start = replica_index * col_share
    root_rows = right_root[0]
    zero_rows = jnp.zeros((col_share, block_order), jnp.float32)
    incoming = lax.all_gather(columns, "replica", axis=0, tiled=True)
    left_acc = zero_rows
    right_part = jnp.einsum("cm,km->ck", columns, incoming, preferred_element_type=jnp.float32)
    right_rows = right_part
    weighted = jnp.dot(root_rows, incoming.astype(jnp.float32), precision=lax.Precision.HIGHEST)
    right_rows, weighted, left_acc = (right_rows, weighted, left_acc)
    partial_left = jnp.einsum("ci,cj->ij", columns, columns, preferred_element_type=jnp.float32)
    summed = lax.psum(partial_left.astype(jnp.bfloat16), "replica").astype(jnp.float32)
    left_rows = lax.dynamic_slice_in_dim(summed, rows_start, col_share, 0)
    transposed = jnp.einsum("jm,im->ji", weighted, left_root[0], precision=lax.Precision.HIGHEST)
    block_rows = jnp.arange(block_order, dtype=jnp.int32)
    keep_mask = (block_rows[None, :] < owned_rows) & (col_index[:, None] < owned_cols)
    result = jnp.where(keep_mask, transposed, jnp.zeros_like(transposed)).astype(jnp.bfloat16)
    returned = lax.all_to_all(
        result.reshape(col_share, fsdp_count, row_share),
        "fsdp",
        split_axis=1,
        concat_axis=1,
        tiled=True,
    )
    update = jnp.einsum("ob,joi->bij", select, returned, preferred_element_type=jnp.float32).astype(
        jnp.bfloat16
    )
    left_new = decay_rate * left_old + ((1.0 - decay_rate) * left_rows)[None]
    right_new = decay_rate * right_old + ((1.0 - decay_rate) * right_rows)[None]
    return (update, left_new, right_new)


def solution(mesh):
    placed = (
        P(None, "fsdp", "replica"),
        P(),
        P(),
        P(),
        P("fsdp", "replica", None),
        P("fsdp", "replica", None),
        P("fsdp", None, None),
        P("fsdp", "replica", None),
    )
    return jax.shard_map(
        body,
        mesh=mesh,
        in_specs=placed,
        out_specs=(
            P(None, "fsdp", "replica"),
            P("fsdp", "replica", None),
            P("fsdp", "replica", None),
        ),
        check_vma=False,
    )
```

profile of v0, /device:TPU:2, one launch (start us, length us, event | category | flops | bytes accessed | tf_op | source)
XLA Modules:
  0.0 167.1 jit_solution(11771236804029011202)
XLA Ops:
  7.2 0.0 copy-start
  7.2 0.9 broadcast_compare_fusion.1
  8.1 0.7 broadcast_compare_fusion
  8.8 1.3 fusion.10
  10.1 0.8 copy.25
  11.0 19.1 %all-to-all-start = ((bf16[96,84,7]{1,2,0:T(8,128)(2,1)}), bf16[96,84,7]{1,2,0:T(8,128)(2,1)S(1)}, u32[]{:S(2)}, u32[]{:S(2)}) async-start(bf16[96,84,7]{1,2,0:T(8,128)(2,1)} %copy.25), calls=%async_computation | async-start | bytes 393216 | tf_op jit(solution)/shard_map/all_to_all | solution.py:27
  30.0 0.0 all-reduce.2.cloned.1.call-start
  30.1 1.3 fusion.25
  31.4 0.7 broadcast_compare_fusion.2
  32.1 0.7 iota_compare_fusion.1
  32.7 12.7 %all-to-all-done = bf16[96,84,7]{1,2,0:T(8,128)(2,1)S(1)} async-done(((bf16[96,84,7]{1,2,0:T(8,128)(2,1)}), bf16[96,84,7]{1,2,0:T(8,128)(2,1)S(1)}, u32[]{:S(2)}, u32[]{:S(2)}) %all-to-all-start) | async-done | bytes 112928 | tf_op jit(solution)/shard_map/all_to_all | solution.py:27
  45.4 0.1 squeeze.9
  45.5 0.1 reshape.93
  45.6 0.2 copy.26
  45.8 30.4 %all-gather = bf16[8,84,672]{2,1,0:T(8,128)(2,1)} all-gather(bf16[1,84,672]{2,1,0:T(8,128)(2,1)S(1)} %copy.26), channel_id=1, replica_groups=mesh['replica'=8,'fsdp'=96] {'replica'}, dimensions={0}, use_global_device_ids=true | all-gather | bytes 1016064 | tf_op jit(solution)/shard_map/all_gather | solution.py:34
  76.1 1.5 reshape.94
  77.6 1.5 convolution_convert_fusion
  79.1 0.0 all-reduce.2.cloned.1.call-update
  79.1 0.0 copy-done.1
  79.1 0.6 fusion.12
  79.8 0.0 copy-done
  79.8 2.6 %fusion.7 = bf16[84,672]{1,0:T(8,128)(2,1)} fusion(f32[672,84]{0,1:T(8,128)S(1)} %fusion.12, f32[1,672,672]{2,1,0:T(8,128)S(1)} %copy-done, pred[672]{0:T(1024)(128)(4,1)S(1)} %iota_compare_fusion.1, pred[84]{0:T(512)(128)(4,1)S(1)} %broadcast_compare_fusion.2), kind=kOutput, calls=%fused_computation.8 | convolution fusion | flops 455366016 | bytes 2145780 | tf_op jit(solution)/shard_map/jm,im->ji/dot_general | solution.py:43
  82.4 1.1 copy.27
  83.5 0.8 reshape.92
  84.3 6.6 %all-to-all-start.1 = ((bf16[84,96,7]{0,2,1:T(8,128)(2,1)}), bf16[84,96,7]{0,2,1:T(8,128)(2,1)S(1)}, u32[]{:S(2)}, u32[]{:S(2)}) async-start(bf16[84,96,7]{0,2,1:T(8,128)(2,1)} %reshape.92), calls=%async_computation.1 | async-start | bytes 393216 | tf_op jit(solution)/shard_map/all_to_all | solution.py:47
  90.8 1.4 fusion.6
  92.3 1.0 copy.32
  93.2 13.1 %all-to-all-done.1 = bf16[84,96,7]{0,2,1:T(8,128)(2,1)S(1)} async-done(((bf16[84,96,7]{0,2,1:T(8,128)(2,1)}), bf16[84,96,7]{0,2,1:T(8,128)(2,1)S(1)}, u32[]{:S(2)}, u32[]{:S(2)}) %all-to-all-start.1) | async-done | bytes 112928 | tf_op jit(solution)/shard_map/all_to_all | solution.py:47
  106.3 0.9 fusion.11
  107.2 51.0 %all-reduce.2.cloned.1.call-done = bf16[672,672]{1,0:T(8,128)(2,1)} async-done(((bf16[672,672]{1,0:T(8,128)(2,1)}), bf16[672,672]{1,0:T(8,128)(2,1)}) %all-reduce.2.cloned.1.call-update) | async-done | bytes 903184 | tf_op jit(solution)/shard_map/psum | solution.py:41
  158.2 1.1 bitcast_add_fusion
  159.3 1.0 copy.31
  (5 shorter events, 0.0 us)
Async XLA Ops:
  7.2 72.6 %copy-start = (f32[1,672,672]{2,1,0:T(8,128)S(1)}, f32[1,672,672]{2,1,0:T(8,128)}, u32[]{:S(2)}) copy-start(f32[1,672,672]{2,1,0:T(8,128)} %param.14) | copy-start | bytes 5419012
  11.0 34.5 %all-to-all-start = ((bf16[96,84,7]{1,2,0:T(8,128)(2,1)}), bf16[96,84,7]{1,2,0:T(8,128)(2,1)S(1)}, u32[]{:S(2)}, u32[]{:S(2)}) async-start(bf16[96,84,7]{1,2,0:T(8,128)(2,1)} %copy.25), calls=%async_computation | async-start | bytes 393216 | tf_op jit(solution)/shard_map/all_to_all | solution.py:27
  30.0 128.2 %all-reduce.2.cloned.1.call-start = ((), (), s32[]{:S(2)}) async-start(), calls=%async_computation.2 | async-start | bytes 2064384 | tf_op jit(solution)/shard_map/psum | solution.py:41
  76.1 3.0 %copy-start.1 = (f32[1,84,672]{2,0,1:T(1,128)S(1)}, f32[1,84,672]{2,0,1:T(1,128)}, u32[]{:S(2)}) copy-start(f32[1,84,672]{2,0,1:T(1,128)} %param.15) | copy-start | bytes 677380
  82.4 23.9 %copy-start.2 = (s32[72]{0:T(128)S(1)}, s32[72]{0:T(128)}, u32[]{:S(2)}) copy-start(s32[72]{0:T(128)} %param.9) | copy-start | bytes 868
  84.3 22.0 %all-to-all-start.1 = ((bf16[84,96,7]{0,2,1:T(8,128)(2,1)}), bf16[84,96,7]{0,2,1:T(8,128)(2,1)S(1)}, u32[]{:S(2)}, u32[]{:S(2)}) async-start(bf16[84,96,7]{0,2,1:T(8,128)(2,1)} %reshape.92), calls=%async_computation.1 | async-start | bytes 393216 | tf_op jit(solution)/shard_map/all_to_all | solution.py:47
Sparse Core Ops, SparseCore 0:
  79.2 78.9 all-reduce.1
where the time goes:
time: 168 us; the launch traced here: 167 us
  waiting for transfers between devices  76.8 us (46%)
  blocking collectives  30.4 us (18%)
  starting transfers between devices  25.7 us (15%)
  between operations  14.2 us (8%)
  matrix products  8.3 us (5%)
  local copies, waits for them, and re-layouts  6.47 us (4%)
  other arithmetic  5.33 us (3%)
    psum x1, waiting for transfers between devices, body(): lax.psum(partial_left.astype(jnp.bfloat16), 'replica').astype(jnp.float32)  51 us
    all_gather x1, blocking collectives, body(): incoming = lax.all_gather(columns, 'replica', axis=0, tiled=True)  30.4 us
    all_to_all x1, starting transfers between devices, body(): lax.all_to_all(outgoing, 'fsdp', split_axis=0, concat_axis=2, tiled=True)[0]  19.1 us
    all_to_all x1, waiting for transfers between devices, body(): lax.all_to_all(result.reshape(col_share, fsdp_count, row_share), 'fsdp',...  13.1 us
    all_to_all x1, waiting for transfers between devices, body(): lax.all_to_all(outgoing, 'fsdp', split_axis=0, concat_axis=2, tiled=True)[0]  12.7 us
    all_to_all x1, starting transfers between devices, body(): lax.all_to_all(result.reshape(col_share, fsdp_count, row_share), 'fsdp',...  6.57 us
    unnamed x11, local copies, waits for them, and re-layouts  3.68 us
  transfers between devices with their start and end apart: 3, of which 3 were waited for; matrix products, arithmetic and copies ran while one was open for 7% of the time, Pallas kernels for 0%

commit v1 on v0

--- a/solution.py
+++ b/solution.py
@@ -30,16 +30,12 @@
     owned_cols = jnp.sum(jnp.where(owned_mask, col_extent, 0))
     rows_start = replica_index * col_share
     root_rows = right_root[0]
-    zero_rows = jnp.zeros((col_share, block_order), jnp.float32)
     incoming = lax.all_gather(columns, "replica", axis=0, tiled=True)
-    left_acc = zero_rows
     right_part = jnp.einsum("cm,km->ck", columns, incoming, preferred_element_type=jnp.float32)
     right_rows = right_part
     weighted = jnp.dot(root_rows, incoming.astype(jnp.float32), precision=lax.Precision.HIGHEST)
-    right_rows, weighted, left_acc = (right_rows, weighted, left_acc)
-    partial_left = jnp.einsum("ci,cj->ij", columns, columns, preferred_element_type=jnp.float32)
-    summed = lax.psum(partial_left.astype(jnp.bfloat16), "replica").astype(jnp.float32)
-    left_rows = lax.dynamic_slice_in_dim(summed, rows_start, col_share, 0)
+    row_slice = lax.dynamic_slice_in_dim(incoming, rows_start, col_share, 1)
+    left_rows = jnp.einsum("ci,cj->ij", row_slice, incoming, preferred_element_type=jnp.float32)
     transposed = jnp.einsum("jm,im->ji", weighted, left_root[0], precision=lax.Precision.HIGHEST)
     block_rows = jnp.arange(block_order, dtype=jnp.int32)
     keep_mask = (block_rows[None, :] < owned_rows) & (col_index[:, None] < owned_cols)

time: 168 us -> 103 us (0.61)
  the two profiles are of different devices: /device:TPU:2 before, /device:TPU:1 now
where the time goes in v1:
time: 103 us; the launch traced here: 102 us
  starting transfers between devices  31.2 us (30%)
  waiting for transfers between devices  26.8 us (26%)
  blocking collectives  24.7 us (24%)
  matrix products  8.22 us (8%)
  local copies, waits for them, and re-layouts  6.39 us (6%)
  other arithmetic  4.24 us (4%)
    all_gather x1, blocking collectives, body(): incoming = lax.all_gather(columns, 'replica', axis=0, tiled=True)  24.7 us
    all_to_all x1, starting transfers between devices, body(): lax.all_to_all(outgoing, 'fsdp', split_axis=0, concat_axis=2, tiled=True)[0]  20 us
    all_to_all x1, waiting for transfers between devices, body(): lax.all_to_all(outgoing, 'fsdp', split_axis=0, concat_axis=2, tiled=True)[0]  13.9 us
    all_to_all x1, waiting for transfers between devices, body(): lax.all_to_all(result.reshape(col_share, fsdp_count, row_share), 'fsdp',...  12.9 us
    all_to_all x1, starting transfers between devices, body(): lax.all_to_all(result.reshape(col_share, fsdp_count, row_share), 'fsdp',...  11.1 us
    unnamed x11, local copies, waits for them, and re-layouts  3.64 us
    dot_general x1, matrix products, body(): jnp.einsum('jm,im->ji', weighted, left_root[0], precision=lax.Precision.H...  2.61 us
  transfers between devices with their start and end apart: 2, of which 2 were waited for; matrix products, arithmetic and copies ran while one was open for 6% of the time, Pallas kernels for 0%

profile of v1, /device:TPU:1, one launch (start us, length us, event | category | flops | bytes accessed | tf_op | source)
XLA Modules:
  0.0 102.2 jit_solution(16915293867604738577)
XLA Ops:
  0.6 0.0 copy-start
  0.7 0.9 broadcast_compare_fusion.1
  1.6 0.7 broadcast_compare_fusion
  2.3 1.3 %fusion.12 = bf16[96,84,7]{0,1,2:T(8,128)(2,1)S(1)} fusion(bf16[72,7,84]{2,0,1:T(8,128)(2,1)} %param.8, pred[72,84]{1,0:T(8,128)(4,1)S(1)} %broadcast_compare_fusion, pred[72,7]{0,1:T(8,128)(4,1)S(1)} %broadcast_compare_fusion.1, s32[72]{0:T(128)} %param.9), kind=kOutput, calls=%fused_computation.12 | convolution fusion | flops 8276544 | bytes 204408 | tf_op jit(solution)/shard_map/ob,bic->oci/dot_general | solution.py:24
  3.6 0.8 copy.25
  4.4 20.0 %all-to-all-start = ((bf16[96,84,7]{1,2,0:T(8,128)(2,1)}), bf16[96,84,7]{1,2,0:T(8,128)(2,1)S(1)}, u32[]{:S(2)}, u32[]{:S(2)}) async-start(bf16[96,84,7]{1,2,0:T(8,128)(2,1)} %copy.25), calls=%async_computation | async-start | bytes 393216 | tf_op jit(solution)/shard_map/all_to_all | solution.py:27
  24.5 1.3 %fusion.28 = (s32[]{:T(128)}, s32[]{:T(128)}) fusion(s32[72]{0:T(128)} %param.11, s32[72]{0:T(128)} %param.9, s32[]{:T(128)S(6)} %axis_index.22, s32[72]{0:T(128)} %param.10), kind=kLoop, calls=%fused_computation.35 | loop fusion | flops 358 | bytes 876 | tf_op jit(solution)/shard_map/reduce_sum | solution.py:30
  25.8 0.7 broadcast_compare_fusion.2
  26.4 0.7 iota_compare_fusion.1
  27.1 13.9 %all-to-all-done = bf16[96,84,7]{1,2,0:T(8,128)(2,1)S(1)} async-done(((bf16[96,84,7]{1,2,0:T(8,128)(2,1)}), bf16[96,84,7]{1,2,0:T(8,128)(2,1)S(1)}, u32[]{:S(2)}, u32[]{:S(2)}) %all-to-all-start) | async-done | bytes 112928 | tf_op jit(solution)/shard_map/all_to_all | solution.py:27
  41.0 0.1 reshape.93
  41.1 0.1 squeeze.9
  41.2 0.2 copy.26
  41.3 24.7 %all-gather = bf16[8,84,672]{2,1,0:T(8,128)(2,1)} all-gather(bf16[1,84,672]{2,1,0:T(8,128)(2,1)S(1)} %copy.26), channel_id=1, replica_groups=mesh['replica'=8,'fsdp'=96] {'replica'}, dimensions={0}, use_global_device_ids=true | all-gather | bytes 1016064 | tf_op jit(solution)/shard_map/all_gather | solution.py:33
  66.0 1.4 %reshape.94 = bf16[672,672]{1,0:T(8,128)(2,1)S(1)} reshape(bf16[8,84,672]{2,1,0:T(8,128)(2,1)} %all-gather) | data formatting | bytes 1806336
  67.4 1.6 %fusion.14 = f32[672,84]{0,1:T(8,128)S(1)} fusion(bf16[672,672]{1,0:T(8,128)(2,1)S(1)} %reshape.94, f32[1,84,672]{2,0,1:T(1,128)} %param.15), kind=kOutput, calls=%fused_computation.14 | convolution fusion | flops 455196672 | bytes 1354752 | tf_op jit(solution)/shard_map/dot_general | solution.py:36
  69.0 0.0 copy-done
  69.0 2.6 %fusion.9 = bf16[84,672]{1,0:T(8,128)(2,1)} fusion(f32[672,84]{0,1:T(8,128)S(1)} %fusion.14, f32[1,672,672]{2,1,0:T(8,128)S(1)} %copy-done, pred[672]{0:T(1024)(128)(4,1)S(1)} %iota_compare_fusion.1, pred[84]{0:T(512)(128)(4,1)S(1)} %broadcast_compare_fusion.2), kind=kOutput, calls=%fused_computation.10 | convolution fusion | flops 455366016 | bytes 2145780 | tf_op jit(solution)/shard_map/jm,im->ji/dot_general | solution.py:39
  71.7 1.1 %copy.27 = bf16[84,672]{0,1:T(8,128)(2,1)S(1)} copy(bf16[84,672]{1,0:T(8,128)(2,1)} %fusion.9) | data formatting | bytes 225792 | tf_op jit(solution)/shard_map/convert_element_type | solution.py:42
  72.7 0.7 reshape.92
  73.5 11.1 %all-to-all-start.1 = ((bf16[84,96,7]{0,2,1:T(8,128)(2,1)}), bf16[84,96,7]{0,2,1:T(8,128)(2,1)S(1)}, u32[]{:S(2)}, u32[]{:S(2)}) async-start(bf16[84,96,7]{0,2,1:T(8,128)(2,1)} %reshape.92), calls=%async_computation.1 | async-start | bytes 393216 | tf_op jit(solution)/shard_map/all_to_all | solution.py:43
  84.6 0.0 copy-start.1
  84.6 0.0 copy-start.2
  84.6 1.4 %fusion.8 = f32[1,84,672]{2,1,0:T(8,128)S(1)} fusion(bf16[84,672]{0,1:T(8,128)(2,1)S(1)} %squeeze.9, bf16[672,672]{1,0:T(8,128)(2,1)S(1)} %reshape.94, f32[1,84,672]{2,0,1:T(1,128)} %param.13), kind=kOutput, calls=%fused_computation.9 | convolution fusion | flops 76035456 | bytes 1467648 | tf_op jit(solution)/shard_map/cm,km->ck/dot_general | solution.py:34
  86.1 1.0 copy.32
  87.0 0.0 copy-done.1
  87.0 0.4 fusion.7
  87.5 1.0 copy.31
  88.4 12.9 %all-to-all-done.1 = bf16[84,96,7]{0,2,1:T(8,128)(2,1)S(1)} async-done(((bf16[84,96,7]{0,2,1:T(8,128)(2,1)}), bf16[84,96,7]{0,2,1:T(8,128)(2,1)S(1)}, u32[]{:S(2)}, u32[]{:S(2)}) %all-to-all-start.1) | async-done | bytes 112928 | tf_op jit(solution)/shard_map/all_to_all | solution.py:43
  101.3 0.0 copy-done.2
  101.3 0.9 fusion.13
  (2 shorter events, 0.0 us)
Async XLA Ops:
  0.6 68.4 %copy-start = (f32[1,672,672]{2,1,0:T(8,128)S(1)}, f32[1,672,672]{2,1,0:T(8,128)}, u32[]{:S(2)}) copy-start(f32[1,672,672]{2,1,0:T(8,128)} %param.14) | copy-start | bytes 5419012
  4.4 36.6 %all-to-all-start = ((bf16[96,84,7]{1,2,0:T(8,128)(2,1)}), bf16[96,84,7]{1,2,0:T(8,128)(2,1)S(1)}, u32[]{:S(2)}, u32[]{:S(2)}) async-start(bf16[96,84,7]{1,2,0:T(8,128)(2,1)} %copy.25), calls=%async_computation | async-start | bytes 393216 | tf_op jit(solution)/shard_map/all_to_all | solution.py:27
  73.5 27.8 %all-to-all-start.1 = ((bf16[84,96,7]{0,2,1:T(8,128)(2,1)}), bf16[84,96,7]{0,2,1:T(8,128)(2,1)S(1)}, u32[]{:S(2)}, u32[]{:S(2)}) async-start(bf16[84,96,7]{0,2,1:T(8,128)(2,1)} %reshape.92), calls=%async_computation.1 | async-start | bytes 393216 | tf_op jit(solution)/shard_map/all_to_all | solution.py:43
  84.6 2.4 %copy-start.1 = (f32[1,84,672]{2,0,1:T(1,128)S(1)}, f32[1,84,672]{2,0,1:T(1,128)}, u32[]{:S(2)}) copy-start(f32[1,84,672]{2,0,1:T(1,128)} %param.12) | copy-start | bytes 677380
  84.6 16.7 %copy-start.2 = (s32[72]{0:T(128)S(1)}, s32[72]{0:T(128)}, u32[]{:S(2)}) copy-start(s32[72]{0:T(128)} %param.9) | copy-start | bytes 868

commit v2 on v1

v2 whole, which is shorter than its diff:
```python
import functools

import jax
import jax.numpy as jnp
from jax import lax
from jax.experimental import pallas as pl
from jax.experimental.pallas import tpu as pltpu
from jax.sharding import PartitionSpec as P

decay_rate = 0.9
lane_count = 128
slot_rows = 8
f32 = jnp.float32
bf16 = jnp.bfloat16
vmem = pl.BlockSpec(memory_space=pltpu.VMEM)
smem = pl.BlockSpec(memory_space=pltpu.SMEM)


def call(kernel, out_shape, in_specs, name, flops, scratch=()):
    return pl.pallas_call(
        kernel,
        out_shape=out_shape,
        in_specs=in_specs,
        out_specs=jax.tree.map(lambda _: vmem, out_shape),
        scratch_shapes=list(scratch),
        compiler_params=pltpu.CompilerParams(vmem_limit_bytes=48 * 2**20),
        cost_estimate=pl.CostEstimate(flops=flops, bytes_accessed=2**20, transcendentals=0),
        name=name,
    )


def iota(shape, dim):
    return lax.broadcasted_iota(jnp.int32, shape, dim)


def rounded_up(value, step):
    return -(-value // step) * step


def one_hot(condition):
    return condition.astype(f32).astype(bf16)


def pack_kernel(owner_ref, grad_ref, wire_ref, slots):
    row_share, block_count, col_share = grad_ref.shape
    fsdp_count = wire_ref.shape[0] // slot_rows
    slots[...] = jnp.zeros_like(slots)
    pick = one_hot(iota((fsdp_count, block_count), 0) == owner_ref[...])
    for i in range(row_share):
        slots[pl.ds(i, fsdp_count, stride=slot_rows), :col_share] = jnp.dot(
            pick, grad_ref[i], preferred_element_type=f32
        )
    wire_ref[...] = slots[...].astype(bf16)


def unpack_kernel(owner_ref, wire_ref, update_ref, slots):
    row_share, block_count, col_share = update_ref.shape
    fsdp_count = wire_ref.shape[0] // slot_rows
    slots[...] = wire_ref[...].astype(f32)
    pick = one_hot(iota((fsdp_count, block_count), 0) == owner_ref[...])
    for i in range(row_share):
        rows = slots[pl.ds(i, fsdp_count, stride=slot_rows), :].astype(bf16)
        picked = lax.dot_general(pick, rows, (((0,), (0,)), ((), ())), preferred_element_type=f32)
        update_ref[i] = picked[:, :col_share].astype(bf16)


def prepare_kernel(row_share, left_ref, right_ref, left_high_ref, left_low_ref, right_ref_out):
    wire_rows, block_order = left_high_ref.shape
    row = iota((wire_rows, block_order), 0)
    place = (row // slot_rows) * row_share + row % slot_rows
    spread = one_hot((place == iota((wire_rows, block_order), 1)) & (row % slot_rows < row_share))
    left = left_ref[...]
    left_high = left.astype(bf16)
    left_low = (left - left_high.astype(f32)).astype(bf16)
    left_high_ref[...] = jnp.dot(spread, left_high, preferred_element_type=f32).astype(bf16)
    left_low_ref[...] = jnp.dot(spread, left_low, preferred_element_type=f32).astype(bf16)
    replica_count, piece_rows, col_share = right_ref_out.shape
    right = right_ref[...]
    right_high = right.astype(bf16).astype(f32)
    right_low = right - right_high
    filler = jnp.zeros((piece_rows // 2 - col_share, col_share), f32)
    for s in range(replica_count):
        part = slice(s * col_share, (s + 1) * col_share)
        right_ref_out[s] = jnp.concatenate(
            [right_high[:, part], filler, right_low[:, part], filler], axis=0
        ).astype(bf16)


def turn_kernel(row_share, extent_ref, wire_ref, columns_ref, slots, rows):
    col_share, block_order = columns_ref.shape
    fsdp_count = wire_ref.shape[0] // slot_rows
    slots[...] = wire_ref[...].astype(f32)
    for i in range(row_share):
        rows[pl.ds(i, fsdp_count, stride=row_share), :] = slots[
            pl.ds(i, fsdp_count, stride=slot_rows), :
        ]
    turned = rows[...].T[:col_share]
    shape = (col_share, block_order)
    keep = (iota(shape, 0) + extent_ref[2] < extent_ref[1]) & (iota(shape, 1) < extent_ref[0])
    columns_ref[...] = jnp.where(keep, turned, 0.0).astype(bf16)


def update_kernel(row_share, extent_ref, block_ref, right_ref, left_high_ref, left_low_ref, wire_ref):
    replica_count, col_share, block_order = block_ref.shape
    half = right_ref.shape[1] // 2
    total = jnp.dot(right_ref[0], block_ref[0], preferred_element_type=f32)
    for s in range(1, replica_count):
        total += jnp.dot(right_ref[s], block_ref[s], preferred_element_type=f32)
    product = total[:half] + total[half:]
    product = jnp.concatenate(
        [product, jnp.zeros((lane_count - half, block_order), f32)], axis=0
    )
    high = product.astype(bf16)
    low = (product - high.astype(f32)).astype(bf16)
    last = (((1,), (1,)), ((), ()))
    first = lax.dot_general(
        left_high_ref[...], jnp.concatenate([high, low], axis=0), last, preferred_element_type=f32
    )
    second = lax.dot_general(left_low_ref[...], high, last, preferred_element_type=f32)
    result = first[:, :lane_count] + first[:, lane_count:] + second
    row = iota(wire_ref.shape, 0)
    lane = iota(wire_ref.shape, 1)
    place = (row // slot_rows) * row_share + row % slot_rows
    keep = (
        (place < extent_ref[0])
        & (row % slot_rows < row_share)
        & (lane + extent_ref[2] < extent_ref[1])
        & (lane < col_share)
    )
    wire_ref[...] = jnp.where(keep, result, 0.0).astype(bf16)


def body(grad, owner, row_extent, col_extent, left_old, right_old, left_root, right_root):
    fsdp_count = lax.axis_size("fsdp")
    fsdp_index = lax.axis_index("fsdp")
    replica_count = lax.axis_size("replica")
    replica_index = lax.axis_index("replica")
    block_count, row_share, col_share = grad.shape
    block_order = row_share * fsdp_count
    wire_shape = (fsdp_count * slot_rows, lane_count)
    wire = jax.ShapeDtypeStruct(wire_shape, bf16)
    slots = pltpu.VMEM(wire_shape, f32)
    owner_row = owner[None, :]

    outgoing = call(pack_kernel, wire, [vmem, vmem], "pack", 2**20, [slots])(
        owner_row, grad.transpose(1, 0, 2)
    )
    received = lax.all_to_all(outgoing, "fsdp", split_axis=0, concat_axis=0, tiled=True)

    owned_mask = owner == fsdp_index
    rows_start = replica_index * col_share
    extents = jnp.stack(
        [
            jnp.sum(jnp.where(owned_mask, row_extent, 0)),
            jnp.sum(jnp.where(owned_mask, col_extent, 0)),
            rows_start,
        ]
    ).astype(jnp.int32)
    spread_shape = jax.ShapeDtypeStruct((wire_shape[0], block_order), bf16)
    half = rounded_up(col_share, 16)
    left_high, left_low, right_pieces = call(
        functools.partial(prepare_kernel, row_share),
        [
            spread_shape,
            spread_shape,
            jax.ShapeDtypeStruct((replica_count, 2 * half, col_share), bf16),
        ],
        [vmem, vmem],
        "prepare",
        2**31,
    )(left_root[0], right_root[0])

    columns = call(
        functools.partial(turn_kernel, row_share),
        jax.ShapeDtypeStruct((col_share, block_order), bf16),
        [smem, vmem],
        "turn",
        2**20,
        [slots, pltpu.VMEM((block_order, lane_count), f32)],
    )(extents, received)
    block = lax.all_gather(columns, "replica", axis=0)
    result = call(
        functools.partial(update_kernel, row_share),
        wire,
        [smem, vmem, vmem, vmem, vmem],
        "update",
        2**30,
    )(extents, block, right_pieces, left_high, left_low)
    returned = lax.all_to_all(result, "fsdp", split_axis=0, concat_axis=0, tiled=True)

    transposed = block.reshape(block_order, block_order)
    row_slice = lax.dynamic_slice_in_dim(transposed, rows_start, col_share, 1)
    left_rows = jnp.einsum("ci,cj->ij", row_slice, transposed, preferred_element_type=f32)
    right_rows = jnp.einsum("cm,km->ck", columns, transposed, preferred_element_type=f32)
    left_new = decay_rate * left_old + ((1.0 - decay_rate) * left_rows)[None]
    right_new = decay_rate * right_old + ((1.0 - decay_rate) * right_rows)[None]

    update = call(
        unpack_kernel,
        jax.ShapeDtypeStruct((row_share, block_count, col_share), bf16),
        [vmem, vmem],
        "unpack",
        2**20,
        [slots],
    )(owner_row, returned)
    return (update.transpose(1, 0, 2), left_new, right_new)


def solution(mesh):
    placed = (
        P(None, "fsdp", "replica"),
        P(),
        P(),
        P(),
        P("fsdp", "replica", None),
        P("fsdp", "replica", None),
        P("fsdp", None, None),
        P("fsdp", "replica", None),
    )
    return jax.shard_map(
        body,
        mesh=mesh,
        in_specs=placed,
        out_specs=(
            P(None, "fsdp", "replica"),
            P("fsdp", "replica", None),
            P("fsdp", "replica", None),
        ),
        check_vma=False,
    )
```

time: 103 us -> 95.4 us (0.926)
  Pallas kernels: 0 us -> 7.66 us
  matrix products: 8.22 us -> 0.86 us
  waiting for transfers between devices: 26.8 us -> 22.3 us
  other arithmetic: 4.24 us -> 2.01 us
  local copies, waits for them, and re-layouts: 6.39 us -> 7.5 us
  blocking collectives: 24.7 us -> 23.6 us
    pallas_call x0 -> x5, Pallas kernels: none -> 7.66 us  [the longest x1 3.1 us: body(): call(functools.partial(update_kernel, row_share), wire, [smem, vmem, vmem...]
    dot_general x6 -> x2, matrix products: 8.22 us -> 0.86 us  [the longest x1 0.44 us: body(): jnp.einsum('cm,km->ck', columns, transposed, preferred_element_type=f32)]
    all_to_all x2, waiting for transfers between devices: 26.8 us -> 22.3 us  [the longest x1 13.5 us: body(): lax.all_to_all(result, 'fsdp', split_axis=0, concat_axis=0, tiled=True)]
    unnamed x11 -> x24, local copies, waits for them, and re-layouts: 3.64 us -> 7.5 us
    lt x4 -> x0, other arithmetic: 2.9 us -> none  [the longest x1 0.87 us: body(): row_index[None, :, None] < row_extent[:, None, None]]
    convert_element_type x2 -> x0, local copies, waits for them, and re-layouts: 1.92 us -> none  [the longest x1 1.07 us: body(): jnp.where(keep_mask, transposed, jnp.zeros_like(transposed))]
    another operation x0 -> x1, other arithmetic: none -> 1.35 us  [body(): jnp.stack([jnp.sum(jnp.where(owned_mask, row_extent, 0)), jnp.sum(jnp.whe...]
    all_gather x1, blocking collectives: 24.7 us -> 23.6 us  [body(): block = lax.all_gather(columns, 'replica', axis=0)]
  transfers between devices with their start and end apart: 2 -> 2, of which waited for: 2 -> 2; matrix products, arithmetic and copies ran while one was open for 6% -> 7% of each run, Pallas kernels for 0% -> 2%
where the time goes in v2:
time: 95.4 us; the launch traced here: 95.1 us
  starting transfers between devices  30.3 us (32%)
  blocking collectives  23.6 us (25%)
  waiting for transfers between devices  22.3 us (23%)
  Pallas kernels  7.66 us (8%)
  local copies, waits for them, and re-layouts  7.5 us (8%)
  other arithmetic  2.01 us (2%)
    all_gather x1, blocking collectives, body(): block = lax.all_gather(columns, 'replica', axis=0)  23.6 us
    all_to_all x1, starting transfers between devices, body(): lax.all_to_all(outgoing, 'fsdp', split_axis=0, concat_axis=0, tiled=True)  20 us
    all_to_all x1, waiting for transfers between devices, body(): lax.all_to_all(result, 'fsdp', split_axis=0, concat_axis=0, tiled=True)  13.5 us
    all_to_all x1, starting transfers between devices, body(): lax.all_to_all(result, 'fsdp', split_axis=0, concat_axis=0, tiled=True)  10.3 us
    all_to_all x1, waiting for transfers between devices, body(): lax.all_to_all(outgoing, 'fsdp', split_axis=0, concat_axis=0, tiled=True)  8.88 us
    unnamed x24, local copies, waits for them, and re-layouts  7.5 us
    pallas_call x1, Pallas kernels, body(): call(functools.partial(update_kernel, row_share), wire, [smem, vmem, vmem...  3.1 us
    pallas_call x1, Pallas kernels, body(): call(functools.partial(prepare_kernel, row_share), [spread_shape, spread_...  2 us
  transfers between devices with their start and end apart: 2, of which 2 were waited for; matrix products, arithmetic and copies ran while one was open for 7% of the time, Pallas kernels for 2%

profile of v2, /device:TPU:1, one launch (start us, length us, event | category | flops | bytes accessed | tf_op | source)
XLA Modules:
  0.0 95.1 jit_solution(7838113803825414858)
XLA Ops:
  0.6 0.0 copy-start.4
  0.6 0.0 copy-start.8
  0.7 0.0 copy-start.9
  0.7 0.0 copy-start.2
  0.7 0.9 copy-done.2
  1.6 0.7 copy-done.3
  2.2 0.9 pack.1
  3.1 20.0 %all-to-all-start = ((bf16[96,8,128]{2,1,0:T(8,128)(2,1)}), bf16[96,8,128]{2,1,0:T(8,128)(2,1)S(1)}, u32[]{:S(2)}, u32[]{:S(2)}) async-start(bf16[96,8,128]{2,1,0:T(8,128)(2,1)} %bitcast.5), calls=%async_computation | async-start | bytes 393216 | tf_op jit(solution)/shard_map/all_to_all | solution.py:148
  23.2 1.0 %copy.31 = f32[1,84,672]{2,1,0:T(8,128)S(1)} copy(f32[1,84,672]{2,0,1:T(1,128)} %param.15) | data formatting | bytes 451584
  24.2 0.0 copy-done.4
  24.2 0.0 copy-done.8
  24.2 0.0 copy-done.9
  24.2 0.7 fusion.5
  24.9 1.4 %pad_add_fusion.extent_ref = s32[3]{0:T(128)S(1)} fusion(s32[1]{0:T(128)} %bitcast.3, s32[1]{0:T(128)} %bitcast.2, s32[1]{0:T(128)} %bitcast.1), kind=kLoop, calls=%fused_computation.14 | loop fusion | flops 6 | bytes 24 | tf_op jit(solution)/shard_map/stack | solution.py:152
  26.2 1.6 %copy-done.5 = f32[1,672,672]{2,1,0:T(8,128)S(1)} copy-done((f32[1,672,672]{2,1,0:T(8,128)S(1)}, f32[1,672,672]{2,1,0:T(8,128)}, u32[]{:S(2)}) %copy-start.5) | copy-done | bytes 1806360
  27.8 2.0 %prepare.1 = (bf16[768,672]{1,0:T(8,128)(2,1)S(1)}, bf16[768,672]{1,0:T(8,128)(2,1)S(1)}, bf16[8,192,84]{2,1,0:T(8,128)(2,1)S(1)}) custom-call(f32[672,672]{1,0:T(8,128)S(1)} %bitcast.33, f32[84,672]{1,0:T(8,128)S(1)} %bitcast.29), custom_call_target="tpu_custom_call" | custom-call | flops 2147483648 | bytes 1048576 | tf_op jit(solution)/shard_map/prepare/pallas_call | solution.py:161
  29.8 1.0 %copy-done = bf16[768,672]{1,0:T(8,128)(2,1)} copy-done((bf16[768,672]{1,0:T(8,128)(2,1)}, bf16[768,672]{1,0:T(8,128)(2,1)S(1)}, u32[]{:S(2)}) %copy-start) | copy-done | bytes 1032216
  30.8 8.9 %all-to-all-done = bf16[96,8,128]{2,1,0:T(8,128)(2,1)S(1)} async-done(((bf16[96,8,128]{2,1,0:T(8,128)(2,1)}), bf16[96,8,128]{2,1,0:T(8,128)(2,1)S(1)}, u32[]{:S(2)}, u32[]{:S(2)}) %all-to-all-start) | async-done | bytes 196640 | tf_op jit(solution)/shard_map/all_to_all | solution.py:148
  39.7 0.7 turn.1
  40.4 23.6 %all-gather.1.block_ref = bf16[8,84,672]{2,1,0:T(8,128)(2,1)S(1)} all-gather(bf16[1,84,672]{2,1,0:T(8,128)(2,1)S(1)} %bitcast.26), channel_id=2, replica_groups=mesh['replica'=8,'fsdp'=96] {'replica'}, dimensions={0}, use_global_device_ids=true | all-gather | bytes 1016064 | tf_op jit(solution)/shard_map/all_gather | solution.py:181
  64.0 3.1 %update.1 = bf16[768,128]{1,0:T(8,128)(2,1)} custom-call(s32[3]{0:T(128)S(1)} %pad_add_fusion.extent_ref, bf16[8,84,672]{2,1,0:T(8,128)(2,1)S(1)} %all-gather.1.block_ref, bf16[8,192,84]{2,1,0:T(8,128)(2,1)S(1)} %get-tuple-element.6.right_ref, bf16[768,672]{1,0:T(8,128)(2,1)S(1)} %get-tuple-element.7.left_high_ref, bf16[768,672]{1,0:T(8,128)(2,1)S(1)} %copy-done.1), custom_call_target="tpu_custom_call" | custom-call | flops 1073741824 | bytes 1048576 | tf_op jit(solution)/shard_map/update/pallas_call | solution.py:182
  67.1 10.3 %all-to-all-start.1 = ((bf16[96,8,128]{2,1,0:T(8,128)(2,1)}), bf16[96,8,128]{2,1,0:T(8,128)(2,1)S(1)}, u32[]{:S(2)}, u32[]{:S(2)}) async-start(bf16[96,8,128]{2,1,0:T(8,128)(2,1)} %bitcast.9), calls=%async_computation.1 | async-start | bytes 393216 | tf_op jit(solution)/shard_map/all_to_all | solution.py:189
  77.4 0.4 reshape.18
  77.9 0.0 copy-done.6
  77.9 0.0 copy-start.7
  77.9 0.4 fusion.2
  78.3 1.0 %copy.21 = f32[1,84,672]{2,0,1:T(1,128)} copy(f32[1,84,672]{2,1,0:T(8,128)S(1)} %fusion.2) | data formatting | bytes 451584
  79.3 0.0 copy-done.7
  79.3 0.4 fusion.3
  79.7 1.0 %copy.22 = f32[1,84,672]{2,0,1:T(1,128)} copy(f32[1,84,672]{2,1,0:T(8,128)S(1)} %fusion.3) | data formatting | bytes 451584
  80.7 13.5 %all-to-all-done.1 = bf16[96,8,128]{2,1,0:T(8,128)(2,1)S(1)} async-done(((bf16[96,8,128]{2,1,0:T(8,128)(2,1)}), bf16[96,8,128]{2,1,0:T(8,128)(2,1)S(1)}, u32[]{:S(2)}, u32[]{:S(2)}) %all-to-all-start.1) | async-done | bytes 196640 | tf_op jit(solution)/shard_map/all_to_all | solution.py:189
  94.1 0.9 unpack.1
  (6 shorter events, 0.0 us)
Async XLA Ops:
  0.6 23.5 %copy-start.4 = (s32[72]{0:T(128)S(1)}, s32[72]{0:T(128)}, u32[]{:S(2)}) copy-start(s32[72]{0:T(128)} %param.9) | copy-start | bytes 868
  0.6 23.5 %copy-start.8 = (s32[72]{0:T(128)S(1)}, s32[72]{0:T(128)}, u32[]{:S(2)}) copy-start(s32[72]{0:T(128)} %param.10) | copy-start | bytes 868
  0.7 23.5 %copy-start.9 = (s32[72]{0:T(128)S(1)}, s32[72]{0:T(128)}, u32[]{:S(2)}) copy-start(s32[72]{0:T(128)} %param.11) | copy-start | bytes 868
  0.7 0.9 copy-start.2
  1.6 0.7 copy-start.3
  3.1 36.6 %all-to-all-start = ((bf16[96,8,128]{2,1,0:T(8,128)(2,1)}), bf16[96,8,128]{2,1,0:T(8,128)(2,1)S(1)}, u32[]{:S(2)}, u32[]{:S(2)}) async-start(bf16[96,8,128]{2,1,0:T(8,128)(2,1)} %bitcast.5), calls=%async_computation | async-start | bytes 393216 | tf_op jit(solution)/shard_map/all_to_all | solution.py:148
  26.2 1.6 %copy-start.5 = (f32[1,672,672]{2,1,0:T(8,128)S(1)}, f32[1,672,672]{2,1,0:T(8,128)}, u32[]{:S(2)}) copy-start(f32[1,672,672]{2,1,0:T(8,128)} %param.14) | copy-start | bytes 5419012
  29.8 1.0 %copy-start = (bf16[768,672]{1,0:T(8,128)(2,1)}, bf16[768,672]{1,0:T(8,128)(2,1)S(1)}, u32[]{:S(2)}) copy-start(bf16[768,672]{1,0:T(8,128)(2,1)S(1)} %get-tuple-element.8.left_low_ref) | copy-start | bytes 3096580
  39.7 24.3 %copy-start.1 = (bf16[768,672]{1,0:T(8,128)(2,1)S(1)}, bf16[768,672]{1,0:T(8,128)(2,1)}, u32[]{:S(2)}) copy-start(bf16[768,672]{1,0:T(8,128)(2,1)} %copy-done) | copy-start | bytes 3096580
  67.1 10.7 %copy-start.6 = (f32[1,84,672]{2,0,1:T(1,128)S(1)}, f32[1,84,672]{2,0,1:T(1,128)}, u32[]{:S(2)}) copy-start(f32[1,84,672]{2,0,1:T(1,128)} %param.12) | copy-start | bytes 677380
  67.1 27.0 %all-to-all-start.1 = ((bf16[96,8,128]{2,1,0:T(8,128)(2,1)}), bf16[96,8,128]{2,1,0:T(8,128)(2,1)S(1)}, u32[]{:S(2)}, u32[]{:S(2)}) async-start(bf16[96,8,128]{2,1,0:T(8,128)(2,1)} %bitcast.9), calls=%async_computation.1 | async-start | bytes 393216 | tf_op jit(solution)/shard_map/all_to_all | solution.py:189
  77.9 1.4 %copy-start.7 = (f32[1,84,672]{2,0,1:T(1,128)S(1)}, f32[1,84,672]{2,0,1:T(1,128)}, u32[]{:S(2)}) copy-start(f32[1,84,672]{2,0,1:T(1,128)} %param.13) | copy-start | bytes 677380

commit v3 on v2

v3 whole, which is shorter than its diff:
```python
import functools

import jax
import jax.numpy as jnp
from jax import lax
from jax.experimental import pallas as pl
from jax.experimental.pallas import tpu as pltpu
from jax.sharding import PartitionSpec as P

decay_rate = 0.9
lane_count = 128
wire_halves = 2
f32 = jnp.float32
bf16 = jnp.bfloat16
vmem = pl.BlockSpec(memory_space=pltpu.VMEM)
hbm = pl.BlockSpec(memory_space=pltpu.HBM)


def call(kernel, out_shape, in_specs, name, flops, scratch=(), out_specs=None):
    return pl.pallas_call(
        kernel,
        out_shape=out_shape,
        in_specs=in_specs,
        out_specs=out_specs or jax.tree.map(lambda _: vmem, out_shape),
        scratch_shapes=list(scratch),
        compiler_params=pltpu.CompilerParams(vmem_limit_bytes=20 * 2**20),
        cost_estimate=pl.CostEstimate(flops=flops, bytes_accessed=2**20, transcendentals=0),
        name=name,
    )


def iota(shape, dim):
    return lax.broadcasted_iota(jnp.int32, shape, dim)


def rounded_up(value, step):
    return -(-value // step) * step


def one_hot(condition):
    return condition.astype(f32).astype(bf16)


def pitch_of(col_share):
    return rounded_up(col_share, 32)


def per_half_of(row_share):
    return -(-row_share // wire_halves)


def wire_lanes(row_share, col_share):
    return rounded_up(per_half_of(row_share) * pitch_of(col_share), lane_count)


def joined(pieces, lanes):
    rows = pieces[0].shape[0]
    width = sum(p.shape[1] for p in pieces)
    if width < lanes:
        pieces = [*pieces, jnp.zeros((rows, lanes - width), pieces[0].dtype)]
    return jnp.concatenate(pieces, axis=1)


def tiles(lanes):
    return [slice(t * lane_count, (t + 1) * lane_count) for t in range(lanes // lane_count)]


def put_half(slots, h, value):
    for t, part in enumerate(tiles(value.shape[1])):
        slots[t, pl.ds(h, value.shape[0], stride=wire_halves), :] = value[:, part]


def get_half(slots, h):
    count = slots.shape[1] // wire_halves
    return jnp.concatenate(
        [slots[t, pl.ds(h, count, stride=wire_halves), :] for t in range(slots.shape[0])], axis=1
    )


def to_wire(slots, wire_ref):
    owners, halves, lanes = wire_ref.shape
    for t, part in enumerate(tiles(lanes)):
        wire_ref[:, :, part] = slots[t].astype(bf16).reshape(owners, halves, lane_count)


def from_wire(slots, wire_ref):
    owners, halves, lanes = wire_ref.shape
    for t, part in enumerate(tiles(lanes)):
        slots[t] = wire_ref[:, :, part].reshape(owners * halves, lane_count).astype(f32)


def pack_kernel(owner_hbm, grad_hbm, wire_ref, owner_ref, grad_ref, slots, sems):
    copies = [
        pltpu.make_async_copy(owner_hbm, owner_ref, sems.at[0]),
        pltpu.make_async_copy(grad_hbm, grad_ref, sems.at[1]),
    ]
    for copy in copies:
        copy.start()
    for copy in copies:
        copy.wait()
    row_share, block_count, col_share = grad_ref.shape
    fsdp_count, _, lanes = wire_ref.shape
    per_half = per_half_of(row_share)
    gap = jnp.zeros((block_count, pitch_of(col_share) - col_share), bf16)
    pick = one_hot(iota((fsdp_count, block_count), 0) == owner_ref[...])
    for h in range(wire_halves):
        pieces = []
        for i in range(h * per_half, min(row_share, (h + 1) * per_half)):
            pieces += [grad_ref[i], gap]
        put_half(
            slots, h, jnp.dot(pick, joined(pieces, lanes), preferred_element_type=f32)
        )
    to_wire(slots, wire_ref)


def unpack_kernel(owner_ref, wire_ref, update_ref, slots):
    row_share, block_count, col_share = update_ref.shape
    fsdp_count = wire_ref.shape[0]
    per_half = per_half_of(row_share)
    pitch = pitch_of(col_share)
    from_wire(slots, wire_ref)
    pick = one_hot(iota((fsdp_count, block_count), 0) == owner_ref[...])
    for h in range(wire_halves):
        rows = get_half(slots, h).astype(bf16)
        picked = lax.dot_general(pick, rows, (((0,), (0,)), ((), ())), preferred_element_type=f32)
        for i in range(h * per_half, min(row_share, (h + 1) * per_half)):
            start = (i - h * per_half) * pitch
            update_ref[i] = picked[:, start : start + col_share].astype(bf16)


def order_matrix(row_share, fsdp_count, forward):
    parts = []
    for i in range(row_share):
        shape = (fsdp_count, row_share * fsdp_count)
        if not forward:
            shape = shape[::-1]
        place, index = (0, 1) if forward else (1, 0)
        parts.append(iota(shape, place) * row_share + i == iota(shape, index))
    parts = [one_hot(p) for p in parts]
    return jnp.concatenate(parts, axis=0 if forward else 1)


def prepare_kernel(row_share, left_ref, right_ref, split_hbm, pieces_ref, split_ref, sem):
    block_order = left_ref.shape[0]
    fsdp_count = block_order // row_share
    rows = order_matrix(row_share, fsdp_count, True)
    cols = order_matrix(row_share, fsdp_count, False)
    left = left_ref[...]
    left_high = left.astype(bf16)
    left_low = (left - left_high.astype(f32)).astype(bf16)
    for n, part in enumerate((left_high, left_low)):
        half_done = jnp.dot(rows, part, preferred_element_type=f32).astype(bf16)
        split_ref[n] = jnp.dot(half_done, cols, preferred_element_type=f32).astype(bf16)
    copy = pltpu.make_async_copy(split_ref, split_hbm, sem.at[0])
    copy.start()
    replica_count, piece_rows, col_share = pieces_ref.shape
    right = right_ref[...]
    right_high = right.astype(bf16).astype(f32)
    right_low = right - right_high
    filler = jnp.zeros((piece_rows // 2 - col_share, col_share), f32)
    for s in range(replica_count):
        part = slice(s * col_share, (s + 1) * col_share)
        pieces_ref[s] = jnp.concatenate(
            [right_high[:, part], filler, right_low[:, part], filler], axis=0
        ).astype(bf16)
    copy.wait()


def owned_extent(owner_ref, extent_ref):
    mine = owner_ref[...] == lax.axis_index("fsdp")
    values = jnp.where(mine, extent_ref[...], 0).astype(f32)
    return jnp.sum(values, axis=1, keepdims=True).astype(jnp.int32)


def turn_kernel(row_share, owner_ref, rows_ref, cols_ref, wire_ref, columns_ref, slots):
    col_share, block_order = columns_ref.shape
    fsdp_count = wire_ref.shape[0]
    per_half = per_half_of(row_share)
    pitch = pitch_of(col_share)
    live_rows = owned_extent(owner_ref, rows_ref)
    live_cols = owned_extent(owner_ref, cols_ref) - lax.axis_index("replica") * col_share
    from_wire(slots, wire_ref)
    shape = (col_share, fsdp_count)
    col_live = iota(shape, 0) < live_cols
    pieces = []
    for h in range(wire_halves):
        turned = get_half(slots, h).T
        for i in range(h * per_half, min(row_share, (h + 1) * per_half)):
            start = (i - h * per_half) * pitch
            keep = col_live & (iota(shape, 1) * row_share + i < live_rows)
            pieces.append(jnp.where(keep, turned[start : start + col_share], 0.0))
    columns_ref[...] = jnp.concatenate(pieces, axis=1).astype(bf16)


def update_kernel(
    row_share, owner_ref, rows_ref, cols_ref, block_ref, right_ref, left_hbm, wire_ref, slots,
    left_ref, sem,
):
    copy = pltpu.make_async_copy(left_hbm, left_ref, sem.at[0])
    copy.start()
    replica_count, col_share, block_order = block_ref.shape
    fsdp_count = block_order // row_share
    per_half = per_half_of(row_share)
    pitch = pitch_of(col_share)
    half = right_ref.shape[1] // 2
    live_rows = owned_extent(owner_ref, rows_ref)
    live_cols = owned_extent(owner_ref, cols_ref) - lax.axis_index("replica") * col_share
    total = jnp.dot(right_ref[0], block_ref[0], preferred_element_type=f32)
    for s in range(1, replica_count):
        total += jnp.dot(right_ref[s], block_ref[s], preferred_element_type=f32)
    product = total[:half] + total[half:]
    product = jnp.concatenate(
        [product, jnp.zeros((lane_count - half, block_order), f32)], axis=0
    )
    high = product.astype(bf16)
    low = (product - high.astype(f32)).astype(bf16)
    last = (((1,), (1,)), ((), ()))
    copy.wait()
    first = lax.dot_general(
        left_ref[0], jnp.concatenate([high, low], axis=0), last, preferred_element_type=f32
    )
    second = lax.dot_general(left_ref[1], high, last, preferred_element_type=f32)
    result = first[:, :lane_count] + first[:, lane_count:] + second
    shape = (fsdp_count, lane_count)
    lane = iota(shape, 1)
    col_live = (lane < live_cols) & (lane < col_share)
    for h in range(wire_halves):
        pieces = []
        for i in range(h * per_half, min(row_share, (h + 1) * per_half)):
            keep = col_live & (iota(shape, 0) * row_share + i < live_rows)
            piece = jnp.where(keep, result[i * fsdp_count : (i + 1) * fsdp_count], 0.0)
            pieces.append(piece[:, :pitch])
        put_half(slots, h, joined(pieces, wire_ref.shape[2]))
    to_wire(slots, wire_ref)


def stats_kernel(row_share, block_ref, columns_ref, after_ref, left_ref, right_ref):
    replica_count, col_share, block_order = block_ref.shape
    fsdp_count = block_order // row_share
    order = order_matrix(row_share, fsdp_count, True)
    rows_start = lax.axis_index("replica") * col_share
    mine = one_hot(
        (iota((block_order, col_share), 0) == iota((block_order, col_share), 1) + rows_start)
    )
    columns = columns_ref[...]
    left = jnp.zeros(left_ref.shape, f32)
    for s in range(replica_count):
        part = jnp.dot(block_ref[s], order, preferred_element_type=f32).astype(bf16)
        picked = jnp.dot(part, mine, preferred_element_type=f32).astype(bf16)
        left += lax.dot_general(
            picked, part, (((0,), (0,)), ((), ())), preferred_element_type=f32
        )
        right_ref[:, s * col_share : (s + 1) * col_share] = lax.dot_general(
            columns, block_ref[s], (((1,), (1,)), ((), ())), preferred_element_type=f32
        )
    left_ref[...] = left


def body(grad, owner, row_extent, col_extent, left_old, right_old, left_root, right_root):
    fsdp_count = lax.axis_size("fsdp")
    replica_count = lax.axis_size("replica")
    block_count, row_share, col_share = grad.shape
    block_order = row_share * fsdp_count
    lanes = wire_lanes(row_share, col_share)
    wire = jax.ShapeDtypeStruct((fsdp_count, wire_halves, lanes), bf16)
    slots = pltpu.VMEM((lanes // lane_count, fsdp_count * wire_halves, lane_count), f32)
    owner_row, live_rows, live_cols = owner[None, :], row_extent[None, :], col_extent[None, :]
    turned_grad = grad.transpose(1, 0, 2)

    def exchange(sent):
        return lax.all_to_all(sent, "fsdp", split_axis=0, concat_axis=0, tiled=True)

    received = exchange(
        call(
            pack_kernel,
            wire,
            [hbm, hbm],
            "pack",
            2**20,
            [
                pltpu.VMEM(owner_row.shape, jnp.int32),
                pltpu.VMEM(turned_grad.shape, bf16),
                slots,
                pltpu.SemaphoreType.DMA((2,)),
            ],
        )(pltpu.with_memory_space_constraint(owner_row, pltpu.HBM),
          pltpu.with_memory_space_constraint(turned_grad, pltpu.HBM))
    )

    root_shape = jax.ShapeDtypeStruct((2, block_order, block_order), bf16)
    half = rounded_up(col_share, 16)
    left_split, right_pieces = call(
        functools.partial(prepare_kernel, row_share),
        [
            root_shape,
            jax.ShapeDtypeStruct((replica_count, 2 * half, col_share), bf16),
        ],
        [vmem, vmem],
        "prepare",
        2**31,
        [pltpu.VMEM(root_shape.shape, bf16), pltpu.SemaphoreType.DMA((1,))],
        [hbm, vmem],
    )(left_root[0], right_root[0])

    columns = call(
        functools.partial(turn_kernel, row_share),
        jax.ShapeDtypeStruct((col_share, block_order), bf16),
        [vmem] * 4,
        "turn",
        2**20,
        [slots],
    )(owner_row, live_rows, live_cols, received)
    block = lax.all_gather(columns, "replica", axis=0)
    result = call(
        functools.partial(update_kernel, row_share),
        wire,
        [vmem] * 5 + [hbm],
        "update",
        2**30,
        [slots, pltpu.VMEM(root_shape.shape, bf16), pltpu.SemaphoreType.DMA((1,))],
    )(
        owner_row,
        live_rows,
        live_cols,
        block,
        right_pieces,
        pltpu.with_memory_space_constraint(left_split, pltpu.HBM),
    )
    returned = exchange(result)

    stat = jax.ShapeDtypeStruct((col_share, block_order), f32)
    left_rows, right_rows = call(
        functools.partial(stats_kernel, row_share),
        [stat, stat],
        [vmem, vmem, hbm],
        "stats",
        2**29,
    )(block, columns, result)
    left_new = decay_rate * left_old + ((1.0 - decay_rate) * left_rows)[None]
    right_new = decay_rate * right_old + ((1.0 - decay_rate) * right_rows)[None]

    update = call(
        unpack_kernel,
        jax.ShapeDtypeStruct((row_share, block_count, col_share), bf16),
        [vmem, vmem],
        "unpack",
        2**20,
        [slots],
    )(owner_row, returned)
    return (update.transpose(1, 0, 2), left_new, right_new)


def solution(mesh):
    placed = (
        P(None, "fsdp", "replica"),
        P(),
        P(),
        P(),
        P("fsdp", "replica", None),
        P("fsdp", "replica", None),
        P("fsdp", None, None),
        P("fsdp", "replica", None),
    )
    return jax.shard_map(
        body,
        mesh=mesh,
        in_specs=placed,
        out_specs=(
            P(None, "fsdp", "replica"),
            P("fsdp", "replica", None),
            P("fsdp", "replica", None),
        ),
        check_vma=False,
    )
```

time: 95.4 us -> 92.6 us (0.971)
  Pallas kernels: 7.66 us -> 15.3 us
  waiting for transfers between devices: 22.3 us -> 15.4 us
  other arithmetic: 2.01 us -> 0.12 us
  local copies, waits for them, and re-layouts: 7.5 us -> 5.81 us
  starting transfers between devices: 30.3 us -> 31.7 us
    pallas_call x3 -> x4, Pallas kernels: 6 us -> 14 us  [the longest x1 4.47 us: body(): call(functools.partial(stats_kernel, row_share), [stat, stat], [vmem, vme...]
    all_to_all x2, waiting for transfers between devices: 22.3 us -> 15.4 us  [exchange(): return lax.all_to_all(sent, 'fsdp', split_axis=0, concat_axis=0, tiled=True)]
    unnamed x24 -> x17, local copies, waits for them, and re-layouts: 7.5 us -> 5.81 us
    all_to_all x2, starting transfers between devices: 30.3 us -> 31.7 us  [exchange(): return lax.all_to_all(sent, 'fsdp', split_axis=0, concat_axis=0, tiled=True)]
    another operation x1 -> x0, other arithmetic: 1.35 us -> none  [body(): jnp.stack([jnp.sum(jnp.where(owned_mask, row_extent, 0)), jnp.sum(jnp.whe...]
  transfers between devices with their start and end apart: 2 -> 2, of which waited for: 2 -> 2; matrix products, arithmetic and copies ran while one was open for 7% -> 3% of each run, Pallas kernels for 2% -> 9%
where the time goes in v3:
time: 92.6 us; the launch traced here: 92.2 us
  starting transfers between devices  31.7 us (34%)
  blocking collectives  23 us (25%)
  waiting for transfers between devices  15.4 us (17%)
  Pallas kernels  15.3 us (17%)
  local copies, waits for them, and re-layouts  5.81 us (6%)
    all_to_all x2, starting transfers between devices, exchange(): return lax.all_to_all(sent, 'fsdp', split_axis=0, concat_axis=0, tiled=True)  31.7 us
    all_gather x1, blocking collectives, body(): block = lax.all_gather(columns, 'replica', axis=0)  23 us
    all_to_all x2, waiting for transfers between devices, exchange(): return lax.all_to_all(sent, 'fsdp', split_axis=0, concat_axis=0, tiled=True)  15.4 us
    unnamed x17, local copies, waits for them, and re-layouts  5.81 us
    pallas_call x1, Pallas kernels, body(): call(functools.partial(stats_kernel, row_share), [stat, stat], [vmem, vme...  4.47 us
    pallas_call x1, Pallas kernels, body(): call(functools.partial(prepare_kernel, row_share), [root_shape, jax.Shape...  4.23 us
    pallas_call x1, Pallas kernels, body(): call(functools.partial(update_kernel, row_share), wire, [vmem] * 5 + [hbm...  3.4 us
    pallas_call x1, Pallas kernels, body(): call(pack_kernel, wire, [hbm, hbm], 'pack', 2 ** 20, [pltpu.VMEM(owner_ro...  1.92 us
  transfers between devices with their start and end apart: 2, of which 2 were waited for; matrix products, arithmetic and copies ran while one was open for 3% of the time, Pallas kernels for 9%

profile of v3, /device:TPU:1, one launch (start us, length us, event | category | flops | bytes accessed | tf_op | source)
XLA Modules:
  0.0 92.2 jit_solution(15659205150680415025)
XLA Ops:
  0.6 1.9 %pack.1 = bf16[96,2,384]{2,1,0:T(2,128)(2,1)} custom-call(s32[1,72]{1,0:T(1,128)} %bitcast.16, bf16[7,72,84]{2,1,0:T(8,128)(2,1)} %bitcast.25), custom_call_target="tpu_custom_call" | custom-call | flops 1048576 | bytes 1048576 | tf_op jit(solution)/shard_map/pack/pallas_call | solution.py:274
  2.6 20.0 %all-to-all-start = ((bf16[96,2,384]{2,1,0:T(2,128)(2,1)}), bf16[96,2,384]{2,1,0:T(2,128)(2,1)S(1)}, u32[]{:S(2)}, u32[]{:S(2)}) async-start(bf16[96,2,384]{2,1,0:T(2,128)(2,1)} %pack.1), calls=%async_computation | async-start | bytes 294912 | tf_op jit(solution)/shard_map/all_to_all | solution.py:271
  22.6 1.0 %copy.27 = f32[1,84,672]{2,1,0:T(8,128)S(1)} copy(f32[1,84,672]{2,0,1:T(1,128)} %param.15) | data formatting | bytes 451584
  23.6 0.0 copy-start.3
  23.6 1.6 %copy-done.3 = f32[1,672,672]{2,1,0:T(8,128)S(1)} copy-done((f32[1,672,672]{2,1,0:T(8,128)S(1)}, f32[1,672,672]{2,1,0:T(8,128)}, u32[]{:S(2)}) %copy-start.3) | copy-done | bytes 1806360
  25.2 0.0 copy-start
  25.2 0.0 copy-start.1
  25.2 0.0 copy-start.2
  25.2 4.2 %prepare.1 = (bf16[2,672,672]{2,1,0:T(8,128)(2,1)S(1)}, bf16[8,192,84]{2,1,0:T(8,128)(2,1)S(1)}) custom-call(f32[672,672]{1,0:T(8,128)S(1)} %bitcast.24, f32[84,672]{1,0:T(8,128)S(1)} %bitcast.15), custom_call_target="tpu_custom_call" | custom-call | flops 2147483648 | bytes 1048576 | tf_op jit(solution)/shard_map/prepare/pallas_call | solution.py:292
  29.4 0.0 copy-start.4
  29.4 1.3 %copy-done.4 = bf16[2,672,672]{2,1,0:T(8,128)(2,1)} copy-done((bf16[2,672,672]{2,1,0:T(8,128)(2,1)}, bf16[2,672,672]{2,1,0:T(8,128)(2,1)S(1)}, u32[]{:S(2)}) %copy-start.4) | copy-done | bytes 1806360
  30.7 6.9 %all-to-all-done.wire_ref = bf16[96,2,384]{2,1,0:T(2,128)(2,1)S(1)} async-done(((bf16[96,2,384]{2,1,0:T(2,128)(2,1)}), bf16[96,2,384]{2,1,0:T(2,128)(2,1)S(1)}, u32[]{:S(2)}, u32[]{:S(2)}) %all-to-all-start) | async-done | bytes 147488 | tf_op jit(solution)/shard_map/all_to_all | solution.py:271
  37.7 0.0 copy-done
  37.7 0.0 copy-done.1
  37.7 0.0 copy-done.2
  37.7 0.3 turn.1.columns_ref
  38.0 23.0 %all-gather.1.block_ref = bf16[8,84,672]{2,1,0:T(8,128)(2,1)S(1)} all-gather(bf16[1,84,672]{2,1,0:T(8,128)(2,1)S(1)} %bitcast.14), channel_id=2, replica_groups=mesh['replica'=8,'fsdp'=96] {'replica'}, dimensions={0}, use_global_device_ids=true | all-gather | bytes 1016064 | tf_op jit(solution)/shard_map/all_gather | solution.py:313
  61.0 3.4 %update.1.after_ref = bf16[96,2,384]{2,1,0:T(2,128)(2,1)} custom-call(s32[1,72]{1,0:T(1,128)S(1)} %bitcast.18, s32[1,72]{1,0:T(1,128)S(1)} %bitcast.21, s32[1,72]{1,0:T(1,128)S(1)} %bitcast.23, bf16[8,84,672]{2,1,0:T(8,128)(2,1)S(1)} %all-gather.1.block_ref, bf16[8,192,84]{2,1,0:T(8,128)(2,1)S(1)} %get-tuple-element.7.right_ref, bf16[2,672,672]{2,1,0:T(8,128)(2,1)} %copy-done.4), custom_call_target="tpu_custom_call" | custom-call | flops 1073741824 | bytes 1048576 | tf_op jit(solution)/shard_map/update/pallas_call | solution.py:314
  64.4 0.0 copy-start.5
  64.4 0.0 copy-start.6
  64.4 11.7 %all-to-all-start.1 = ((bf16[96,2,384]{2,1,0:T(2,128)(2,1)}), bf16[96,2,384]{2,1,0:T(2,128)(2,1)S(1)}, u32[]{:S(2)}, u32[]{:S(2)}) async-start(bf16[96,2,384]{2,1,0:T(2,128)(2,1)} %update.1.after_ref), calls=%async_computation.1 | async-start | bytes 294912 | tf_op jit(solution)/shard_map/all_to_all | solution.py:271
  76.1 4.5 %stats.1 = (f32[84,672]{1,0:T(8,128)S(1)}, f32[84,672]{1,0:T(8,128)S(1)}) custom-call(bf16[8,84,672]{2,1,0:T(8,128)(2,1)S(1)} %all-gather.1.block_ref, bf16[84,672]{1,0:T(8,128)(2,1)S(1)} %turn.1.columns_ref, bf16[96,2,384]{2,1,0:T(2,128)(2,1)} %update.1.after_ref), custom_call_target="tpu_custom_call" | custom-call | flops 536870912 | bytes 1048576 | tf_op jit(solution)/shard_map/stats/pallas_call | solution.py:332
  80.6 0.0 copy-done.5
  80.6 0.0 copy-done.6
  80.6 0.1 bitcast_add_fusion
  80.7 1.0 %copy.18 = f32[1,84,672]{2,0,1:T(1,128)} copy(f32[1,84,672]{2,1,0:T(8,128)S(1)} %get-tuple-element.17) | data formatting | bytes 451584
  81.7 1.0 %copy.17 = f32[1,84,672]{2,0,1:T(1,128)} copy(f32[1,84,672]{2,1,0:T(8,128)S(1)} %get-tuple-element.18) | data formatting | bytes 451584
  82.7 8.5 %all-to-all-done.1.wire_ref = bf16[96,2,384]{2,1,0:T(2,128)(2,1)S(1)} async-done(((bf16[96,2,384]{2,1,0:T(2,128)(2,1)}), bf16[96,2,384]{2,1,0:T(2,128)(2,1)S(1)}, u32[]{:S(2)}, u32[]{:S(2)}) %all-to-all-start.1) | async-done | bytes 147488 | tf_op jit(solution)/shard_map/all_to_all | solution.py:271
  91.2 1.0 %unpack.1 = bf16[7,72,84]{2,1,0:T(8,128)(2,1)} custom-call(s32[1,72]{1,0:T(1,128)S(1)} %bitcast.19, bf16[96,2,384]{2,1,0:T(2,128)(2,1)S(1)} %all-to-all-done.1.wire_ref), custom_call_target="tpu_custom_call" | custom-call | flops 1048576 | bytes 1048576 | tf_op jit(solution)/shard_map/unpack/pallas_call | solution.py:342
Async XLA Ops:
  2.6 35.1 %all-to-all-start = ((bf16[96,2,384]{2,1,0:T(2,128)(2,1)}), bf16[96,2,384]{2,1,0:T(2,128)(2,1)S(1)}, u32[]{:S(2)}, u32[]{:S(2)}) async-start(bf16[96,2,384]{2,1,0:T(2,128)(2,1)} %pack.1), calls=%async_computation | async-start | bytes 294912 | tf_op jit(solution)/shard_map/all_to_all | solution.py:271
  23.6 1.6 %copy-start.3 = (f32[1,672,672]{2,1,0:T(8,128)S(1)}, f32[1,672,672]{2,1,0:T(8,128)}, u32[]{:S(2)}) copy-start(f32[1,672,672]{2,1,0:T(8,128)} %param.14) | copy-start | bytes 5419012
  25.2 12.5 %copy-start = (s32[72]{0:T(128)S(1)}, s32[72]{0:T(128)}, u32[]{:S(2)}) copy-start(s32[72]{0:T(128)} %param.9) | copy-start | bytes 868
  25.2 12.5 %copy-start.1 = (s32[72]{0:T(128)S(1)}, s32[72]{0:T(128)}, u32[]{:S(2)}) copy-start(s32[72]{0:T(128)} %param.10) | copy-start | bytes 868
  25.2 12.5 %copy-start.2 = (s32[72]{0:T(128)S(1)}, s32[72]{0:T(128)}, u32[]{:S(2)}) copy-start(s32[72]{0:T(128)} %param.11) | copy-start | bytes 868
  29.4 1.3 %copy-start.4 = (bf16[2,672,672]{2,1,0:T(8,128)(2,1)}, bf16[2,672,672]{2,1,0:T(8,128)(2,1)S(1)}, u32[]{:S(2)}) copy-start(bf16[2,672,672]{2,1,0:T(8,128)(2,1)S(1)} %get-tuple-element.8.left_hbm) | copy-start | bytes 5419012
  64.4 16.2 %copy-start.5 = (f32[1,84,672]{2,0,1:T(1,128)S(1)}, f32[1,84,672]{2,0,1:T(1,128)}, u32[]{:S(2)}) copy-start(f32[1,84,672]{2,0,1:T(1,128)} %param.13) | copy-start | bytes 677380
  64.4 16.2 %copy-start.6 = (f32[1,84,672]{2,0,1:T(1,128)S(1)}, f32[1,84,672]{2,0,1:T(1,128)}, u32[]{:S(2)}) copy-start(f32[1,84,672]{2,0,1:T(1,128)} %param.12) | copy-start | bytes 677380
  64.4 26.7 %all-to-all-start.1 = ((bf16[96,2,384]{2,1,0:T(2,128)(2,1)}), bf16[96,2,384]{2,1,0:T(2,128)(2,1)S(1)}, u32[]{:S(2)}, u32[]{:S(2)}) async-start(bf16[96,2,384]{2,1,0:T(2,128)(2,1)} %update.1.after_ref), calls=%async_computation.1 | async-start | bytes 294912 | tf_op jit(solution)/shard_map/all_to_all | solution.py:271

commit v4 on v3

--- a/solution.py
+++ b/solution.py
@@ -140,7 +140,9 @@
     return jnp.concatenate(parts, axis=0 if forward else 1)
 
 
-def prepare_kernel(row_share, left_ref, right_ref, split_hbm, pieces_ref, split_ref, sem):
+def prepare_kernel(
+    row_share, left_ref, right_ref, left_high_ref, left_low_hbm, pieces_ref, left_low_ref, sem
+):
     block_order = left_ref.shape[0]
     fsdp_count = block_order // row_share
     rows = order_matrix(row_share, fsdp_count, True)
@@ -148,10 +150,10 @@
     left = left_ref[...]
     left_high = left.astype(bf16)
     left_low = (left - left_high.astype(f32)).astype(bf16)
-    for n, part in enumerate((left_high, left_low)):
+    for part, ref in ((left_low, left_low_ref), (left_high, left_high_ref)):
         half_done = jnp.dot(rows, part, preferred_element_type=f32).astype(bf16)
-        split_ref[n] = jnp.dot(half_done, cols, preferred_element_type=f32).astype(bf16)
-    copy = pltpu.make_async_copy(split_ref, split_hbm, sem.at[0])
+        ref[...] = jnp.dot(half_done, cols, preferred_element_type=f32).astype(bf16)
+    copy = pltpu.make_async_copy(left_low_ref, left_low_hbm, sem.at[0])
     copy.start()
     replica_count, piece_rows, col_share = pieces_ref.shape
     right = right_ref[...]
@@ -193,10 +195,10 @@
 
 
 def update_kernel(
-    row_share, owner_ref, rows_ref, cols_ref, block_ref, right_ref, left_hbm, wire_ref, slots,
-    left_ref, sem,
+    row_share, owner_ref, rows_ref, cols_ref, block_ref, right_ref, left_high_ref, left_low_hbm,
+    wire_ref, slots, left_low_ref, sem,
 ):
-    copy = pltpu.make_async_copy(left_hbm, left_ref, sem.at[0])
+    copy = pltpu.make_async_copy(left_low_hbm, left_low_ref, sem.at[0])
     copy.start()
     replica_count, col_share, block_order = block_ref.shape
     fsdp_count = block_order // row_share
@@ -215,11 +217,11 @@
     high = product.astype(bf16)
     low = (product - high.astype(f32)).astype(bf16)
     last = (((1,), (1,)), ((), ()))
+    first = lax.dot_general(
+        left_high_ref[...], jnp.concatenate([high, low], axis=0), last, preferred_element_type=f32
+    )
     copy.wait()
-    first = lax.dot_general(
-        left_ref[0], jnp.concatenate([high, low], axis=0), last, preferred_element_type=f32
-    )
-    second = lax.dot_general(left_ref[1], high, last, preferred_element_type=f32)
+    second = lax.dot_general(left_low_ref[...], high, last, preferred_element_type=f32)
     result = first[:, :lane_count] + first[:, lane_count:] + second
     shape = (fsdp_count, lane_count)
     lane = iota(shape, 1)
@@ -262,7 +264,7 @@
     block_count, row_share, col_share = grad.shape
     block_order = row_share * fsdp_count
     lanes = wire_lanes(row_share, col_share)
-    wire = jax.ShapeDtypeStruct((fsdp_count, wire_halves, lanes), bf16)
+    wire = pltpu.VMEM((fsdp_count, wire_halves, lanes), bf16)
     slots = pltpu.VMEM((lanes // lane_count, fsdp_count * wire_halves, lane_count), f32)
     owner_row, live_rows, live_cols = owner[None, :], row_extent[None, :], col_extent[None, :]
     turned_grad = grad.transpose(1, 0, 2)
@@ -287,19 +289,20 @@
           pltpu.with_memory_space_constraint(turned_grad, pltpu.HBM))
     )
 
-    root_shape = jax.ShapeDtypeStruct((2, block_order, block_order), bf16)
+    root_shape = (block_order, block_order)
     half = rounded_up(col_share, 16)
-    left_split, right_pieces = call(
+    left_high, left_low, right_pieces = call(
         functools.partial(prepare_kernel, row_share),
         [
-            root_shape,
+            jax.ShapeDtypeStruct(root_shape, bf16),
+            pltpu.HBM(root_shape, bf16),
             jax.ShapeDtypeStruct((replica_count, 2 * half, col_share), bf16),
         ],
         [vmem, vmem],
         "prepare",
         2**31,
-        [pltpu.VMEM(root_shape.shape, bf16), pltpu.SemaphoreType.DMA((1,))],
-        [hbm, vmem],
+        [pltpu.VMEM(root_shape, bf16), pltpu.SemaphoreType.DMA((1,))],
+        [vmem, hbm, vmem],
     )(left_root[0], right_root[0])
 
     columns = call(
@@ -314,17 +317,18 @@
     result = call(
         functools.partial(update_kernel, row_share),
         wire,
-        [vmem] * 5 + [hbm],
+        [vmem] * 6 + [hbm],
         "update",
         2**30,
-        [slots, pltpu.VMEM(root_shape.shape, bf16), pltpu.SemaphoreType.DMA((1,))],
+        [slots, pltpu.VMEM(root_shape, bf16), pltpu.SemaphoreType.DMA((1,))],
     )(
         owner_row,
         live_rows,
         live_cols,
         block,
         right_pieces,
-        pltpu.with_memory_space_constraint(left_split, pltpu.HBM),
+        left_high,
+        pltpu.with_memory_space_constraint(left_low, pltpu.HBM),
     )
     returned = exchange(result)
 

time: 92.6 us -> 91.7 us (level)
  waiting for transfers between devices: 15.4 us -> 17.7 us
  local copies, waits for them, and re-layouts: 5.81 us -> 4.5 us
  Pallas kernels: 15.3 us -> 14.2 us
    all_to_all x2, waiting for transfers between devices: 15.4 us -> 17.7 us  [exchange(): return lax.all_to_all(sent, 'fsdp', split_axis=0, concat_axis=0, tiled=True)]
    unnamed x17 -> x15, local copies, waits for them, and re-layouts: 5.81 us -> 4.5 us
    pallas_call x2, Pallas kernels: 7.63 us -> 6.47 us  [the longest x1 3.57 us: body(): call(functools.partial(prepare_kernel, row_share), [jax.ShapeDtypeStruct(...]
where the time goes in v4:
time: 91.7 us; the launch traced here: 91.4 us
  starting transfers between devices  31.2 us (34%)
  blocking collectives  23 us (25%)
  waiting for transfers between devices  17.7 us (19%)
  Pallas kernels  14.2 us (15%)
  local copies, waits for them, and re-layouts  4.5 us (5%)
    all_to_all x2, starting transfers between devices, exchange(): return lax.all_to_all(sent, 'fsdp', split_axis=0, concat_axis=0, tiled=True)  31.2 us
    all_gather x1, blocking collectives, body(): block = lax.all_gather(columns, 'replica', axis=0)  23 us
    all_to_all x2, waiting for transfers between devices, exchange(): return lax.all_to_all(sent, 'fsdp', split_axis=0, concat_axis=0, tiled=True)  17.7 us
    unnamed x15, local copies, waits for them, and re-layouts  4.5 us
    pallas_call x1, Pallas kernels, body(): call(functools.partial(stats_kernel, row_share), [stat, stat], [vmem, vme...  4.45 us
    pallas_call x1, Pallas kernels, body(): call(functools.partial(prepare_kernel, row_share), [jax.ShapeDtypeStruct(...  3.57 us
    pallas_call x1, Pallas kernels, body(): call(functools.partial(update_kernel, row_share), wire, [vmem] * 6 + [hbm...  2.89 us
    pallas_call x1, Pallas kernels, body(): call(pack_kernel, wire, [hbm, hbm], 'pack', 2 ** 20, [pltpu.VMEM(owner_ro...  1.92 us
  transfers between devices with their start and end apart: 2, of which 2 were waited for; matrix products, arithmetic and copies ran while one was open for 3% of the time, Pallas kernels for 9%

profile of v4, /device:TPU:1, one launch (start us, length us, event | category | flops | bytes accessed | tf_op | source)
XLA Modules:
  0.0 91.4 jit_solution(3753703241363962103)
XLA Ops:
  0.6 1.9 %pack.1 = bf16[96,2,384]{2,1,0:T(2,128)(2,1)} custom-call(s32[1,72]{1,0:T(1,128)} %bitcast.16, bf16[7,72,84]{2,1,0:T(8,128)(2,1)} %bitcast.25), custom_call_target="tpu_custom_call" | custom-call | flops 1048576 | bytes 1048576 | tf_op jit(solution)/shard_map/pack/pallas_call | solution.py:276
  2.6 20.0 %all-to-all-start = ((bf16[96,2,384]{2,1,0:T(2,128)(2,1)}), bf16[96,2,384]{2,1,0:T(2,128)(2,1)S(1)}, u32[]{:S(2)}, u32[]{:S(2)}) async-start(bf16[96,2,384]{2,1,0:T(2,128)(2,1)} %pack.1), calls=%async_computation | async-start | bytes 294912 | tf_op jit(solution)/shard_map/all_to_all | solution.py:273
  22.6 1.0 %copy.27 = f32[1,84,672]{2,1,0:T(8,128)S(1)} copy(f32[1,84,672]{2,0,1:T(1,128)} %param.15) | data formatting | bytes 451584
  23.6 0.0 copy-start.3
  23.6 1.6 %copy-done.3 = f32[1,672,672]{2,1,0:T(8,128)S(1)} copy-done((f32[1,672,672]{2,1,0:T(8,128)S(1)}, f32[1,672,672]{2,1,0:T(8,128)}, u32[]{:S(2)}) %copy-start.3) | copy-done | bytes 1806360
  25.2 0.0 copy-start
  25.2 0.0 copy-start.1
  25.2 0.0 copy-start.2
  25.2 3.6 %prepare.1 = (bf16[672,672]{1,0:T(8,128)(2,1)S(1)}, bf16[672,672]{1,0:T(8,128)(2,1)}, bf16[8,192,84]{2,1,0:T(8,128)(2,1)S(1)}) custom-call(f32[672,672]{1,0:T(8,128)S(1)} %bitcast.24, f32[84,672]{1,0:T(8,128)S(1)} %bitcast.15), custom_call_target="tpu_custom_call" | custom-call | flops 2147483648 | bytes 1048576 | tf_op jit(solution)/shard_map/prepare/pallas_call | solution.py:294
  28.7 8.9 %all-to-all-done.wire_ref = bf16[96,2,384]{2,1,0:T(2,128)(2,1)S(1)} async-done(((bf16[96,2,384]{2,1,0:T(2,128)(2,1)}), bf16[96,2,384]{2,1,0:T(2,128)(2,1)S(1)}, u32[]{:S(2)}, u32[]{:S(2)}) %all-to-all-start) | async-done | bytes 147488 | tf_op jit(solution)/shard_map/all_to_all | solution.py:273
  37.7 0.0 copy-done
  37.7 0.0 copy-done.1
  37.7 0.0 copy-done.2
  37.7 0.3 turn.1.columns_ref
  38.0 23.0 %all-gather.1.block_ref = bf16[8,84,672]{2,1,0:T(8,128)(2,1)S(1)} all-gather(bf16[1,84,672]{2,1,0:T(8,128)(2,1)S(1)} %bitcast.14), channel_id=2, replica_groups=mesh['replica'=8,'fsdp'=96] {'replica'}, dimensions={0}, use_global_device_ids=true | all-gather | bytes 1016064 | tf_op jit(solution)/shard_map/all_gather | solution.py:316
  61.0 2.9 %update.1.after_ref = bf16[96,2,384]{2,1,0:T(2,128)(2,1)} custom-call(s32[1,72]{1,0:T(1,128)S(1)} %bitcast.18, s32[1,72]{1,0:T(1,128)S(1)} %bitcast.21, s32[1,72]{1,0:T(1,128)S(1)} %bitcast.23, bf16[8,84,672]{2,1,0:T(8,128)(2,1)S(1)} %all-gather.1.block_ref, bf16[8,192,84]{2,1,0:T(8,128)(2,1)S(1)} %get-tuple-element.8.right_ref, ...), custom_call_target="tpu_custom_call" | custom-call | flops 1073741824 | bytes 1048576 | tf_op jit(solution)/shard_map/update/pallas_call | solution.py:317
  63.9 0.0 copy-start.4
  63.9 0.0 copy-start.5
  63.9 11.2 %all-to-all-start.1 = ((bf16[96,2,384]{2,1,0:T(2,128)(2,1)}), bf16[96,2,384]{2,1,0:T(2,128)(2,1)S(1)}, u32[]{:S(2)}, u32[]{:S(2)}) async-start(bf16[96,2,384]{2,1,0:T(2,128)(2,1)} %update.1.after_ref), calls=%async_computation.1 | async-start | bytes 294912 | tf_op jit(solution)/shard_map/all_to_all | solution.py:273
  75.1 4.5 %stats.1 = (f32[84,672]{1,0:T(8,128)S(1)}, f32[84,672]{1,0:T(8,128)S(1)}) custom-call(bf16[8,84,672]{2,1,0:T(8,128)(2,1)S(1)} %all-gather.1.block_ref, bf16[84,672]{1,0:T(8,128)(2,1)S(1)} %turn.1.columns_ref, bf16[96,2,384]{2,1,0:T(2,128)(2,1)} %update.1.after_ref), custom_call_target="tpu_custom_call" | custom-call | flops 536870912 | bytes 1048576 | tf_op jit(solution)/shard_map/stats/pallas_call | solution.py:336
  79.6 0.0 copy-done.4
  79.6 0.0 copy-done.5
  79.6 0.1 bitcast_add_fusion
  79.7 1.0 %copy.18 = f32[1,84,672]{2,0,1:T(1,128)} copy(f32[1,84,672]{2,1,0:T(8,128)S(1)} %get-tuple-element.19) | data formatting | bytes 451584
  80.7 1.0 %copy.17 = f32[1,84,672]{2,0,1:T(1,128)} copy(f32[1,84,672]{2,1,0:T(8,128)S(1)} %get-tuple-element.20) | data formatting | bytes 451584
  81.6 8.8 %all-to-all-done.1.wire_ref = bf16[96,2,384]{2,1,0:T(2,128)(2,1)S(1)} async-done(((bf16[96,2,384]{2,1,0:T(2,128)(2,1)}), bf16[96,2,384]{2,1,0:T(2,128)(2,1)S(1)}, u32[]{:S(2)}, u32[]{:S(2)}) %all-to-all-start.1) | async-done | bytes 147488 | tf_op jit(solution)/shard_map/all_to_all | solution.py:273
  90.4 1.0 %unpack.1 = bf16[7,72,84]{2,1,0:T(8,128)(2,1)} custom-call(s32[1,72]{1,0:T(1,128)S(1)} %bitcast.19, bf16[96,2,384]{2,1,0:T(2,128)(2,1)S(1)} %all-to-all-done.1.wire_ref), custom_call_target="tpu_custom_call" | custom-call | flops 1048576 | bytes 1048576 | tf_op jit(solution)/shard_map/unpack/pallas_call | solution.py:346
Async XLA Ops:
  2.6 35.1 %all-to-all-start = ((bf16[96,2,384]{2,1,0:T(2,128)(2,1)}), bf16[96,2,384]{2,1,0:T(2,128)(2,1)S(1)}, u32[]{:S(2)}, u32[]{:S(2)}) async-start(bf16[96,2,384]{2,1,0:T(2,128)(2,1)} %pack.1), calls=%async_computation | async-start | bytes 294912 | tf_op jit(solution)/shard_map/all_to_all | solution.py:273
  23.6 1.6 %copy-start.3 = (f32[1,672,672]{2,1,0:T(8,128)S(1)}, f32[1,672,672]{2,1,0:T(8,128)}, u32[]{:S(2)}) copy-start(f32[1,672,672]{2,1,0:T(8,128)} %param.14) | copy-start | bytes 5419012
  25.2 12.5 %copy-start = (s32[72]{0:T(128)S(1)}, s32[72]{0:T(128)}, u32[]{:S(2)}) copy-start(s32[72]{0:T(128)} %param.9) | copy-start | bytes 868
  25.2 12.5 %copy-start.1 = (s32[72]{0:T(128)S(1)}, s32[72]{0:T(128)}, u32[]{:S(2)}) copy-start(s32[72]{0:T(128)} %param.10) | copy-start | bytes 868
  25.2 12.5 %copy-start.2 = (s32[72]{0:T(128)S(1)}, s32[72]{0:T(128)}, u32[]{:S(2)}) copy-start(s32[72]{0:T(128)} %param.11) | copy-start | bytes 868
  63.9 15.7 %copy-start.4 = (f32[1,84,672]{2,0,1:T(1,128)S(1)}, f32[1,84,672]{2,0,1:T(1,128)}, u32[]{:S(2)}) copy-start(f32[1,84,672]{2,0,1:T(1,128)} %param.13) | copy-start | bytes 677380
  63.9 15.7 %copy-start.5 = (f32[1,84,672]{2,0,1:T(1,128)S(1)}, f32[1,84,672]{2,0,1:T(1,128)}, u32[]{:S(2)}) copy-start(f32[1,84,672]{2,0,1:T(1,128)} %param.12) | copy-start | bytes 677380
  63.9 26.5 %all-to-all-start.1 = ((bf16[96,2,384]{2,1,0:T(2,128)(2,1)}), bf16[96,2,384]{2,1,0:T(2,128)(2,1)S(1)}, u32[]{:S(2)}, u32[]{:S(2)}) async-start(bf16[96,2,384]{2,1,0:T(2,128)(2,1)} %update.1.after_ref), calls=%async_computation.1 | async-start | bytes 294912 | tf_op jit(solution)/shard_map/all_to_all | solution.py:273

commit v5 on v4

--- a/solution.py
+++ b/solution.py
@@ -71,7 +71,7 @@
 
 
 def get_half(slots, h):
-    count = slots.shape[1] // wire_halves
+    count = (slots.shape[1] - 8) // wire_halves
     return jnp.concatenate(
         [slots[t, pl.ds(h, count, stride=wire_halves), :] for t in range(slots.shape[0])], axis=1
     )
@@ -80,13 +80,15 @@
 def to_wire(slots, wire_ref):
     owners, halves, lanes = wire_ref.shape
     for t, part in enumerate(tiles(lanes)):
-        wire_ref[:, :, part] = slots[t].astype(bf16).reshape(owners, halves, lane_count)
+        rows = slots[t, : owners * halves].astype(bf16)
+        wire_ref[:, :, part] = rows.reshape(owners, halves, lane_count)
 
 
 def from_wire(slots, wire_ref):
     owners, halves, lanes = wire_ref.shape
     for t, part in enumerate(tiles(lanes)):
-        slots[t] = wire_ref[:, :, part].reshape(owners * halves, lane_count).astype(f32)
+        rows = wire_ref[:, :, part].reshape(owners * halves, lane_count)
+        slots[t, : owners * halves] = rows.astype(f32)
 
 
 def pack_kernel(owner_hbm, grad_hbm, wire_ref, owner_ref, grad_ref, slots, sems):
@@ -128,6 +130,14 @@
             update_ref[i] = picked[:, start : start + col_share].astype(bf16)
 
 
+def folded(columns):
+    third = columns.shape[0] // 3
+    middle = columns.shape[1] // 2
+    rest = columns[2 * third :]
+    rest = jnp.concatenate([rest[:, :middle], rest[:, middle:]], axis=0)
+    return jnp.concatenate([columns[: 2 * third], rest], axis=1)
+
+
 def order_matrix(row_share, fsdp_count, forward):
     parts = []
     for i in range(row_share):
@@ -141,7 +151,8 @@
 
 
 def prepare_kernel(
-    row_share, left_ref, right_ref, left_high_ref, left_low_hbm, pieces_ref, left_low_ref, sem
+    row_share, left_ref, right_ref, left_high_ref, left_low_hbm, top_ref, rest_ref, left_low_ref,
+    sem,
 ):
     block_order = left_ref.shape[0]
     fsdp_count = block_order // row_share
@@ -155,16 +166,26 @@
         ref[...] = jnp.dot(half_done, cols, preferred_element_type=f32).astype(bf16)
     copy = pltpu.make_async_copy(left_low_ref, left_low_hbm, sem.at[0])
     copy.start()
-    replica_count, piece_rows, col_share = pieces_ref.shape
+    col_share = right_ref.shape[0]
+    third = col_share // 3
+    replica_count = block_order // col_share
     right = right_ref[...]
     right_high = right.astype(bf16).astype(f32)
     right_low = right - right_high
-    filler = jnp.zeros((piece_rows // 2 - col_share, col_share), f32)
-    for s in range(replica_count):
-        part = slice(s * col_share, (s + 1) * col_share)
-        pieces_ref[s] = jnp.concatenate(
-            [right_high[:, part], filler, right_low[:, part], filler], axis=0
-        ).astype(bf16)
+    filler = jnp.zeros((top_ref.shape[0] // 2 - col_share, block_order), f32)
+    both = jnp.concatenate([right_high, filler, right_low, filler], axis=0)
+    tops, uppers, lowers = [], [], []
+    empty = jnp.zeros((both.shape[0], third), f32)
+    for n in range(replica_count):
+        start = n * col_share
+        tops.append(both[:, start : start + 2 * third])
+        rest = both[:, start + 2 * third : start + col_share]
+        uppers += [rest, empty]
+        lowers += [empty, rest]
+    top_ref[...] = jnp.concatenate(tops, axis=1).astype(bf16)
+    rest_ref[...] = jnp.concatenate(
+        [jnp.concatenate(uppers, axis=1), jnp.concatenate(lowers, axis=1)], axis=0
+    ).astype(bf16)
     copy.wait()
 
 
@@ -174,7 +195,9 @@
     return jnp.sum(values, axis=1, keepdims=True).astype(jnp.int32)
 
 
-def turn_kernel(row_share, owner_ref, rows_ref, cols_ref, wire_ref, columns_ref, slots):
+def turn_kernel(
+    row_share, owner_ref, rows_ref, cols_ref, wire_ref, columns_ref, folded_ref, slots
+):
     col_share, block_order = columns_ref.shape
     fsdp_count = wire_ref.shape[0]
     per_half = per_half_of(row_share)
@@ -191,26 +214,29 @@
             start = (i - h * per_half) * pitch
             keep = col_live & (iota(shape, 1) * row_share + i < live_rows)
             pieces.append(jnp.where(keep, turned[start : start + col_share], 0.0))
-    columns_ref[...] = jnp.concatenate(pieces, axis=1).astype(bf16)
+    columns = jnp.concatenate(pieces, axis=1)
+    columns_ref[...] = columns.astype(bf16)
+    folded_ref[...] = folded(columns).astype(bf16)
 
 
 def update_kernel(
-    row_share, owner_ref, rows_ref, cols_ref, block_ref, right_ref, left_high_ref, left_low_hbm,
-    wire_ref, slots, left_low_ref, sem,
+    row_share, col_share, owner_ref, rows_ref, cols_ref, block_ref, top_ref, rest_ref,
+    left_high_ref, left_low_hbm, wire_ref, slots, left_low_ref, sem,
 ):
     copy = pltpu.make_async_copy(left_low_hbm, left_low_ref, sem.at[0])
     copy.start()
-    replica_count, col_share, block_order = block_ref.shape
+    block_order = left_high_ref.shape[0]
     fsdp_count = block_order // row_share
     per_half = per_half_of(row_share)
     pitch = pitch_of(col_share)
-    half = right_ref.shape[1] // 2
+    half = top_ref.shape[0] // 2
     live_rows = owned_extent(owner_ref, rows_ref)
     live_cols = owned_extent(owner_ref, cols_ref) - lax.axis_index("replica") * col_share
-    total = jnp.dot(right_ref[0], block_ref[0], preferred_element_type=f32)
-    for s in range(1, replica_count):
-        total += jnp.dot(right_ref[s], block_ref[s], preferred_element_type=f32)
+    rest = jnp.dot(rest_ref[...], block_ref[:, block_order:], preferred_element_type=f32)
+    rest = rest.reshape(4, half, rest.shape[1])
+    total = jnp.dot(top_ref[...], block_ref[:, :block_order], preferred_element_type=f32)
     product = total[:half] + total[half:]
+    product += jnp.concatenate([rest[0] + rest[1], rest[2] + rest[3]], axis=1)
     product = jnp.concatenate(
         [product, jnp.zeros((lane_count - half, block_order), f32)], axis=0
     )
@@ -237,23 +263,38 @@
 
 
 def stats_kernel(row_share, block_ref, columns_ref, after_ref, left_ref, right_ref):
-    replica_count, col_share, block_order = block_ref.shape
-    fsdp_count = block_order // row_share
-    order = order_matrix(row_share, fsdp_count, True)
+    col_share, block_order = columns_ref.shape
+    third = col_share // 3
+    middle = block_order // 2
+    replica_count = block_order // col_share
+    order = order_matrix(row_share, block_order // row_share, True)
     rows_start = lax.axis_index("replica") * col_share
     mine = one_hot(
-        (iota((block_order, col_share), 0) == iota((block_order, col_share), 1) + rows_start)
-    )
+        iota((block_order, col_share), 0) == iota((block_order, col_share), 1) + rows_start
+    )
+    top = block_ref[:, :block_order]
+    rest = block_ref[:, block_order:]
+    natural_top = jnp.dot(top, order, preferred_element_type=f32).astype(bf16)
+    split = (replica_count, 2 * third, block_order)
+    upper = jnp.dot(rest, order[:middle], preferred_element_type=f32).reshape(split)
+    lower = jnp.dot(rest, order[middle:], preferred_element_type=f32).reshape(split)
     columns = columns_ref[...]
-    left = jnp.zeros(left_ref.shape, f32)
-    for s in range(replica_count):
-        part = jnp.dot(block_ref[s], order, preferred_element_type=f32).astype(bf16)
-        picked = jnp.dot(part, mine, preferred_element_type=f32).astype(bf16)
-        left += lax.dot_general(
-            picked, part, (((0,), (0,)), ((), ())), preferred_element_type=f32
-        )
-        right_ref[:, s * col_share : (s + 1) * col_share] = lax.dot_general(
-            columns, block_ref[s], (((1,), (1,)), ((), ())), preferred_element_type=f32
+    last = (((1,), (1,)), ((), ()))
+    with_top = lax.dot_general(columns, top, last, preferred_element_type=f32)
+    with_upper = lax.dot_general(columns[:, :middle], rest, last, preferred_element_type=f32)
+    with_lower = lax.dot_general(columns[:, middle:], rest, last, preferred_element_type=f32)
+    first = (((0,), (0,)), ((), ()))
+    picked = jnp.dot(natural_top, mine, preferred_element_type=f32).astype(bf16)
+    left = lax.dot_general(picked, natural_top, first, preferred_element_type=f32)
+    for n in range(replica_count):
+        natural = (upper[n, :third] + lower[n, third:]).astype(bf16)
+        picked = jnp.dot(natural, mine, preferred_element_type=f32).astype(bf16)
+        left += lax.dot_general(picked, natural, first, preferred_element_type=f32)
+        start = n * col_share
+        held = n * 2 * third
+        right_ref[:, start : start + 2 * third] = with_top[:, held : held + 2 * third]
+        right_ref[:, start + 2 * third : start + col_share] = (
+            with_upper[:, held : held + third] + with_lower[:, held + third : held + 2 * third]
         )
     left_ref[...] = left
 
@@ -265,7 +306,7 @@
     block_order = row_share * fsdp_count
     lanes = wire_lanes(row_share, col_share)
     wire = pltpu.VMEM((fsdp_count, wire_halves, lanes), bf16)
-    slots = pltpu.VMEM((lanes // lane_count, fsdp_count * wire_halves, lane_count), f32)
+    slots = pltpu.VMEM((lanes // lane_count, fsdp_count * wire_halves + 8, lane_count), f32)
     owner_row, live_rows, live_cols = owner[None, :], row_extent[None, :], col_extent[None, :]
     turned_grad = grad.transpose(1, 0, 2)
 
@@ -291,33 +332,38 @@
 
     root_shape = (block_order, block_order)
     half = rounded_up(col_share, 16)
-    left_high, left_low, right_pieces = call(
+    folded_shape = (col_share // 3 * 2, block_order // 2 * 3)
+    left_high, left_low, right_top, right_rest = call(
         functools.partial(prepare_kernel, row_share),
         [
             jax.ShapeDtypeStruct(root_shape, bf16),
             pltpu.HBM(root_shape, bf16),
-            jax.ShapeDtypeStruct((replica_count, 2 * half, col_share), bf16),
+            jax.ShapeDtypeStruct((2 * half, folded_shape[0] * replica_count), bf16),
+            jax.ShapeDtypeStruct((4 * half, folded_shape[0] * replica_count), bf16),
         ],
         [vmem, vmem],
         "prepare",
         2**31,
         [pltpu.VMEM(root_shape, bf16), pltpu.SemaphoreType.DMA((1,))],
-        [vmem, hbm, vmem],
+        [vmem, hbm, vmem, vmem],
     )(left_root[0], right_root[0])
 
-    columns = call(
+    columns, sent = call(
         functools.partial(turn_kernel, row_share),
-        jax.ShapeDtypeStruct((col_share, block_order), bf16),
+        [
+            jax.ShapeDtypeStruct((col_share, block_order), bf16),
+            jax.ShapeDtypeStruct(folded_shape, bf16),
+        ],
         [vmem] * 4,
         "turn",
         2**20,
         [slots],
     )(owner_row, live_rows, live_cols, received)
-    block = lax.all_gather(columns, "replica", axis=0)
+    block = lax.all_gather(sent, "replica", axis=0, tiled=True)
     result = call(
-        functools.partial(update_kernel, row_share),
+        functools.partial(update_kernel, row_share, col_share),
         wire,
-        [vmem] * 6 + [hbm],
+        [vmem] * 7 + [hbm],
         "update",
         2**30,
         [slots, pltpu.VMEM(root_shape, bf16), pltpu.SemaphoreType.DMA((1,))],
@@ -326,7 +372,8 @@
         live_rows,
         live_cols,
         block,
-        right_pieces,
+        right_top,
+        right_rest,
         left_high,
         pltpu.with_memory_space_constraint(left_low, pltpu.HBM),
     )

time: 91.7 us -> 92.4 us (level)
    pallas_call x1, Pallas kernels: 4.45 us -> 3.34 us  [body(): call(functools.partial(stats_kernel, row_share), [stat, stat], [vmem, vme...]
    pallas_call x2, Pallas kernels: 3.2 us -> 4.17 us  [the longest x1 3.74 us: body(): call(functools.partial(update_kernel, row_share, col_share), wire, [vmem]...]
  transfers between devices with their start and end apart: 2 -> 2, of which waited for: 2 -> 2; matrix products, arithmetic and copies ran while one was open for 3% -> 3% of each run, Pallas kernels for 9% -> 8%
where the time goes in v5:
time: 92.4 us; the launch traced here: 92 us
  starting transfers between devices  31 us (34%)
  blocking collectives  22.8 us (25%)
  waiting for transfers between devices  18.1 us (20%)
  Pallas kernels  14.8 us (16%)
  local copies, waits for them, and re-layouts  4.5 us (5%)
    all_to_all x2, starting transfers between devices, exchange(): return lax.all_to_all(sent, 'fsdp', split_axis=0, concat_axis=0, tiled=True)  31 us
    all_gather x1, blocking collectives, body(): block = lax.all_gather(sent, 'replica', axis=0, tiled=True)  22.8 us
    all_to_all x2, waiting for transfers between devices, exchange(): return lax.all_to_all(sent, 'fsdp', split_axis=0, concat_axis=0, tiled=True)  18.1 us
    unnamed x15, local copies, waits for them, and re-layouts  4.5 us
    pallas_call x1, Pallas kernels, body(): call(functools.partial(prepare_kernel, row_share), [jax.ShapeDtypeStruct(...  4.3 us
    pallas_call x1, Pallas kernels, body(): call(functools.partial(update_kernel, row_share, col_share), wire, [vmem]...  3.74 us
    pallas_call x1, Pallas kernels, body(): call(functools.partial(stats_kernel, row_share), [stat, stat], [vmem, vme...  3.34 us
    pallas_call x1, Pallas kernels, body(): call(pack_kernel, wire, [hbm, hbm], 'pack', 2 ** 20, [pltpu.VMEM(owner_ro...  1.92 us
  transfers between devices with their start and end apart: 2, of which 2 were waited for; matrix products, arithmetic and copies ran while one was open for 3% of the time, Pallas kernels for 8%

profile of v5, /device:TPU:1, one launch (start us, length us, event | category | flops | bytes accessed | tf_op | source)
XLA Modules:
  0.0 92.0 jit_solution(15650748762233806865)
XLA Ops:
  0.6 1.9 %pack.1 = bf16[96,2,384]{2,1,0:T(2,128)(2,1)} custom-call(s32[1,72]{1,0:T(1,128)} %bitcast.14, bf16[7,72,84]{2,1,0:T(8,128)(2,1)} %bitcast.23), custom_call_target="tpu_custom_call" | custom-call | flops 1048576 | bytes 1048576 | tf_op jit(solution)/shard_map/pack/pallas_call | solution.py:317
  2.6 20.0 %all-to-all-start = ((bf16[96,2,384]{2,1,0:T(2,128)(2,1)}), bf16[96,2,384]{2,1,0:T(2,128)(2,1)S(1)}, u32[]{:S(2)}, u32[]{:S(2)}) async-start(bf16[96,2,384]{2,1,0:T(2,128)(2,1)} %pack.1), calls=%async_computation | async-start | bytes 294912 | tf_op jit(solution)/shard_map/all_to_all | solution.py:314
  22.6 1.0 %copy.23 = f32[1,84,672]{2,1,0:T(8,128)S(1)} copy(f32[1,84,672]{2,0,1:T(1,128)} %param.15) | data formatting | bytes 451584
  23.6 0.0 copy-start.3
  23.6 1.6 %copy-done.3 = f32[1,672,672]{2,1,0:T(8,128)S(1)} copy-done((f32[1,672,672]{2,1,0:T(8,128)S(1)}, f32[1,672,672]{2,1,0:T(8,128)}, u32[]{:S(2)}) %copy-start.3) | copy-done | bytes 1806360
  25.2 0.0 copy-start
  25.2 0.0 copy-start.1
  25.2 0.0 copy-start.2
  25.2 4.3 %prepare.1 = (bf16[672,672]{1,0:T(8,128)(2,1)S(1)}, bf16[672,672]{1,0:T(8,128)(2,1)}, bf16[192,448]{1,0:T(8,128)(2,1)S(1)}, bf16[384,448]{1,0:T(8,128)(2,1)S(1)}) custom-call(f32[672,672]{1,0:T(8,128)S(1)} %bitcast.22, f32[84,672]{1,0:T(8,128)S(1)} %bitcast.13), custom_call_target="tpu_custom_call" | custom-call | flops 2147483648 | bytes 1048576 | tf_op jit(solution)/shard_map/prepare/pallas_call | solution.py:336
  29.5 8.2 %all-to-all-done.wire_ref = bf16[96,2,384]{2,1,0:T(2,128)(2,1)S(1)} async-done(((bf16[96,2,384]{2,1,0:T(2,128)(2,1)}), bf16[96,2,384]{2,1,0:T(2,128)(2,1)S(1)}, u32[]{:S(2)}, u32[]{:S(2)}) %all-to-all-start) | async-done | bytes 147488 | tf_op jit(solution)/shard_map/all_to_all | solution.py:314
  37.7 0.0 copy-done
  37.7 0.0 copy-done.1
  37.7 0.0 copy-done.2
  37.7 0.4 turn.1
  38.1 22.8 %all_gather.3.block_ref = bf16[448,1008]{1,0:T(8,128)(2,1)S(1)} all-gather(bf16[56,1008]{1,0:T(8,128)(2,1)S(1)} %get-tuple-element.11), channel_id=1, replica_groups=mesh['replica'=8,'fsdp'=96] {'replica'}, dimensions={0}, use_global_device_ids=true | all-gather | bytes 1016064 | tf_op jit(solution)/shard_map/all_gather | solution.py:362
  60.9 3.7 %update.1.after_ref = bf16[96,2,384]{2,1,0:T(2,128)(2,1)} custom-call(s32[1,72]{1,0:T(1,128)S(1)} %bitcast.16, s32[1,72]{1,0:T(1,128)S(1)} %bitcast.19, s32[1,72]{1,0:T(1,128)S(1)} %bitcast.21, bf16[448,1008]{1,0:T(8,128)(2,1)S(1)} %all_gather.3.block_ref, bf16[192,448]{1,0:T(8,128)(2,1)S(1)} %get-tuple-element.12.top_ref, ...), custom_call_target="tpu_custom_call" | custom-call | flops 1073741824 | bytes 1048576 | tf_op jit(solution)/shard_map/update/pallas_call | solution.py:363
  64.7 0.0 copy-start.4
  64.7 0.0 copy-start.5
  64.7 11.0 %all-to-all-start.1 = ((bf16[96,2,384]{2,1,0:T(2,128)(2,1)}), bf16[96,2,384]{2,1,0:T(2,128)(2,1)S(1)}, u32[]{:S(2)}, u32[]{:S(2)}) async-start(bf16[96,2,384]{2,1,0:T(2,128)(2,1)} %update.1.after_ref), calls=%async_computation.1 | async-start | bytes 294912 | tf_op jit(solution)/shard_map/all_to_all | solution.py:314
  75.7 3.3 %stats.1 = (f32[84,672]{1,0:T(8,128)S(1)}, f32[84,672]{1,0:T(8,128)S(1)}) custom-call(bf16[448,1008]{1,0:T(8,128)(2,1)S(1)} %all_gather.3.block_ref, bf16[84,672]{1,0:T(8,128)(2,1)S(1)} %get-tuple-element.16.columns_ref, bf16[96,2,384]{2,1,0:T(2,128)(2,1)} %update.1.after_ref), custom_call_target="tpu_custom_call" | custom-call | flops 536870912 | bytes 1048576 | tf_op jit(solution)/shard_map/stats/pallas_call | solution.py:383
  79.0 0.0 copy-done.4
  79.0 0.0 copy-done.5
  79.1 0.1 bitcast_add_fusion
  79.2 1.0 %copy.14 = f32[1,84,672]{2,0,1:T(1,128)} copy(f32[1,84,672]{2,1,0:T(8,128)S(1)} %get-tuple-element.22) | data formatting | bytes 451584
  80.1 1.0 %copy.13 = f32[1,84,672]{2,0,1:T(1,128)} copy(f32[1,84,672]{2,1,0:T(8,128)S(1)} %get-tuple-element.23) | data formatting | bytes 451584
  81.1 9.9 %all-to-all-done.1.wire_ref = bf16[96,2,384]{2,1,0:T(2,128)(2,1)S(1)} async-done(((bf16[96,2,384]{2,1,0:T(2,128)(2,1)}), bf16[96,2,384]{2,1,0:T(2,128)(2,1)S(1)}, u32[]{:S(2)}, u32[]{:S(2)}) %all-to-all-start.1) | async-done | bytes 147488 | tf_op jit(solution)/shard_map/all_to_all | solution.py:314
  91.0 1.0 %unpack.1 = bf16[7,72,84]{2,1,0:T(8,128)(2,1)} custom-call(s32[1,72]{1,0:T(1,128)S(1)} %bitcast.17, bf16[96,2,384]{2,1,0:T(2,128)(2,1)S(1)} %all-to-all-done.1.wire_ref), custom_call_target="tpu_custom_call" | custom-call | flops 1048576 | bytes 1048576 | tf_op jit(solution)/shard_map/unpack/pallas_call | solution.py:393
Async XLA Ops:
  2.6 35.1 %all-to-all-start = ((bf16[96,2,384]{2,1,0:T(2,128)(2,1)}), bf16[96,2,384]{2,1,0:T(2,128)(2,1)S(1)}, u32[]{:S(2)}, u32[]{:S(2)}) async-start(bf16[96,2,384]{2,1,0:T(2,128)(2,1)} %pack.1), calls=%async_computation | async-start | bytes 294912 | tf_op jit(solution)/shard_map/all_to_all | solution.py:314
  23.6 1.6 %copy-start.3 = (f32[1,672,672]{2,1,0:T(8,128)S(1)}, f32[1,672,672]{2,1,0:T(8,128)}, u32[]{:S(2)}) copy-start(f32[1,672,672]{2,1,0:T(8,128)} %param.14) | copy-start | bytes 5419012
  25.2 12.5 %copy-start = (s32[72]{0:T(128)S(1)}, s32[72]{0:T(128)}, u32[]{:S(2)}) copy-start(s32[72]{0:T(128)} %param.9) | copy-start | bytes 868
  25.2 12.5 %copy-start.1 = (s32[72]{0:T(128)S(1)}, s32[72]{0:T(128)}, u32[]{:S(2)}) copy-start(s32[72]{0:T(128)} %param.10) | copy-start | bytes 868
  25.2 12.5 %copy-start.2 = (s32[72]{0:T(128)S(1)}, s32[72]{0:T(128)}, u32[]{:S(2)}) copy-start(s32[72]{0:T(128)} %param.11) | copy-start | bytes 868
  64.7 14.4 %copy-start.4 = (f32[1,84,672]{2,0,1:T(1,128)S(1)}, f32[1,84,672]{2,0,1:T(1,128)}, u32[]{:S(2)}) copy-start(f32[1,84,672]{2,0,1:T(1,128)} %param.13) | copy-start | bytes 677380
  64.7 14.4 %copy-start.5 = (f32[1,84,672]{2,0,1:T(1,128)S(1)}, f32[1,84,672]{2,0,1:T(1,128)}, u32[]{:S(2)}) copy-start(f32[1,84,672]{2,0,1:T(1,128)} %param.12) | copy-start | bytes 677380
  64.7 26.3 %all-to-all-start.1 = ((bf16[96,2,384]{2,1,0:T(2,128)(2,1)}), bf16[96,2,384]{2,1,0:T(2,128)(2,1)S(1)}, u32[]{:S(2)}, u32[]{:S(2)}) async-start(bf16[96,2,384]{2,1,0:T(2,128)(2,1)} %update.1.after_ref), calls=%async_computation.1 | async-start | bytes 294912 | tf_op jit(solution)/shard_map/all_to_all | solution.py:314

commit v6 on v4

--- a/solution.py
+++ b/solution.py
@@ -71,7 +71,7 @@
 
 
 def get_half(slots, h):
-    count = slots.shape[1] // wire_halves
+    count = (slots.shape[1] - 8) // wire_halves
     return jnp.concatenate(
         [slots[t, pl.ds(h, count, stride=wire_halves), :] for t in range(slots.shape[0])], axis=1
     )
@@ -80,13 +80,15 @@
 def to_wire(slots, wire_ref):
     owners, halves, lanes = wire_ref.shape
     for t, part in enumerate(tiles(lanes)):
-        wire_ref[:, :, part] = slots[t].astype(bf16).reshape(owners, halves, lane_count)
+        rows = slots[t, : owners * halves].astype(bf16)
+        wire_ref[:, :, part] = rows.reshape(owners, halves, lane_count)
 
 
 def from_wire(slots, wire_ref):
     owners, halves, lanes = wire_ref.shape
     for t, part in enumerate(tiles(lanes)):
-        slots[t] = wire_ref[:, :, part].reshape(owners * halves, lane_count).astype(f32)
+        rows = wire_ref[:, :, part].reshape(owners * halves, lane_count)
+        slots[t, : owners * halves] = rows.astype(f32)
 
 
 def pack_kernel(owner_hbm, grad_hbm, wire_ref, owner_ref, grad_ref, slots, sems):
@@ -150,21 +152,23 @@
     left = left_ref[...]
     left_high = left.astype(bf16)
     left_low = (left - left_high.astype(f32)).astype(bf16)
-    for part, ref in ((left_low, left_low_ref), (left_high, left_high_ref)):
-        half_done = jnp.dot(rows, part, preferred_element_type=f32).astype(bf16)
-        ref[...] = jnp.dot(half_done, cols, preferred_element_type=f32).astype(bf16)
+    half_done = jnp.dot(rows, left_low, preferred_element_type=f32).astype(bf16)
+    left_low_ref[...] = jnp.dot(half_done, cols, preferred_element_type=f32).astype(bf16)
     copy = pltpu.make_async_copy(left_low_ref, left_low_hbm, sem.at[0])
     copy.start()
-    replica_count, piece_rows, col_share = pieces_ref.shape
+    half_done = jnp.dot(rows, left_high, preferred_element_type=f32).astype(bf16)
+    left_high_ref[...] = jnp.dot(half_done, cols, preferred_element_type=f32).astype(bf16)
+    col_share = right_ref.shape[0]
+    replica_count = block_order // col_share
     right = right_ref[...]
     right_high = right.astype(bf16).astype(f32)
-    right_low = right - right_high
-    filler = jnp.zeros((piece_rows // 2 - col_share, col_share), f32)
-    for s in range(replica_count):
-        part = slice(s * col_share, (s + 1) * col_share)
-        pieces_ref[s] = jnp.concatenate(
-            [right_high[:, part], filler, right_low[:, part], filler], axis=0
-        ).astype(bf16)
+    filler = jnp.zeros((pieces_ref.shape[0] // 2 - col_share, block_order), f32)
+    both = jnp.concatenate([right_high, filler, right - right_high, filler], axis=0)
+    gap = jnp.zeros((both.shape[0], pieces_ref.shape[1] // replica_count - col_share), f32)
+    spaced = []
+    for n in range(replica_count):
+        spaced += [both[:, n * col_share : (n + 1) * col_share], gap]
+    pieces_ref[...] = jnp.concatenate(spaced, axis=1).astype(bf16)
     copy.wait()
 
 
@@ -174,42 +178,40 @@
     return jnp.sum(values, axis=1, keepdims=True).astype(jnp.int32)
 
 
-def turn_kernel(row_share, owner_ref, rows_ref, cols_ref, wire_ref, columns_ref, slots):
-    col_share, block_order = columns_ref.shape
+def turn_kernel(row_share, col_share, owner_ref, rows_ref, cols_ref, wire_ref, columns_ref, slots):
+    held_rows = columns_ref.shape[0]
     fsdp_count = wire_ref.shape[0]
     per_half = per_half_of(row_share)
     pitch = pitch_of(col_share)
     live_rows = owned_extent(owner_ref, rows_ref)
     live_cols = owned_extent(owner_ref, cols_ref) - lax.axis_index("replica") * col_share
     from_wire(slots, wire_ref)
-    shape = (col_share, fsdp_count)
-    col_live = iota(shape, 0) < live_cols
+    shape = (held_rows, fsdp_count)
+    col_live = (iota(shape, 0) < live_cols) & (iota(shape, 0) < col_share)
     pieces = []
     for h in range(wire_halves):
         turned = get_half(slots, h).T
         for i in range(h * per_half, min(row_share, (h + 1) * per_half)):
             start = (i - h * per_half) * pitch
             keep = col_live & (iota(shape, 1) * row_share + i < live_rows)
-            pieces.append(jnp.where(keep, turned[start : start + col_share], 0.0))
+            pieces.append(jnp.where(keep, turned[start : start + held_rows], 0.0))
     columns_ref[...] = jnp.concatenate(pieces, axis=1).astype(bf16)
 
 
 def update_kernel(
-    row_share, owner_ref, rows_ref, cols_ref, block_ref, right_ref, left_high_ref, left_low_hbm,
-    wire_ref, slots, left_low_ref, sem,
+    row_share, col_share, owner_ref, rows_ref, cols_ref, block_ref, right_ref, left_high_ref,
+    left_low_hbm, wire_ref, slots, left_low_ref, sem,
 ):
     copy = pltpu.make_async_copy(left_low_hbm, left_low_ref, sem.at[0])
     copy.start()
-    replica_count, col_share, block_order = block_ref.shape
+    block_order = block_ref.shape[1]
     fsdp_count = block_order // row_share
     per_half = per_half_of(row_share)
     pitch = pitch_of(col_share)
-    half = right_ref.shape[1] // 2
+    half = right_ref.shape[0] // 2
     live_rows = owned_extent(owner_ref, rows_ref)
     live_cols = owned_extent(owner_ref, cols_ref) - lax.axis_index("replica") * col_share
-    total = jnp.dot(right_ref[0], block_ref[0], preferred_element_type=f32)
-    for s in range(1, replica_count):
-        total += jnp.dot(right_ref[s], block_ref[s], preferred_element_type=f32)
+    total = jnp.dot(right_ref[...], block_ref[...], preferred_element_type=f32)
     product = total[:half] + total[half:]
     product = jnp.concatenate(
         [product, jnp.zeros((lane_count - half, block_order), f32)], axis=0
@@ -236,26 +238,23 @@
     to_wire(slots, wire_ref)
 
 
-def stats_kernel(row_share, block_ref, columns_ref, after_ref, left_ref, right_ref):
-    replica_count, col_share, block_order = block_ref.shape
-    fsdp_count = block_order // row_share
-    order = order_matrix(row_share, fsdp_count, True)
+def stats_kernel(row_share, col_share, block_ref, columns_ref, after_ref, left_ref, right_ref):
+    held_rows, block_order = columns_ref.shape
+    order = order_matrix(row_share, block_order // row_share, True)
     rows_start = lax.axis_index("replica") * col_share
-    mine = one_hot(
-        (iota((block_order, col_share), 0) == iota((block_order, col_share), 1) + rows_start)
-    )
-    columns = columns_ref[...]
-    left = jnp.zeros(left_ref.shape, f32)
-    for s in range(replica_count):
-        part = jnp.dot(block_ref[s], order, preferred_element_type=f32).astype(bf16)
-        picked = jnp.dot(part, mine, preferred_element_type=f32).astype(bf16)
-        left += lax.dot_general(
-            picked, part, (((0,), (0,)), ((), ())), preferred_element_type=f32
-        )
-        right_ref[:, s * col_share : (s + 1) * col_share] = lax.dot_general(
-            columns, block_ref[s], (((1,), (1,)), ((), ())), preferred_element_type=f32
-        )
-    left_ref[...] = left
+    shape = (block_order, col_share)
+    mine = one_hot(iota(shape, 0) == iota(shape, 1) + rows_start)
+    natural = jnp.dot(block_ref[...], order, preferred_element_type=f32).astype(bf16)
+    picked = jnp.dot(natural, mine, preferred_element_type=f32).astype(bf16)
+    left_ref[...] = lax.dot_general(
+        picked, natural, (((0,), (0,)), ((), ())), preferred_element_type=f32
+    )
+    right = lax.dot_general(
+        columns_ref[...], block_ref[...], (((1,), (1,)), ((), ())), preferred_element_type=f32
+    )[:col_share]
+    for n in range(block_order // col_share):
+        held = right[:, n * held_rows : n * held_rows + col_share]
+        right_ref[:, n * col_share : (n + 1) * col_share] = held
 
 
 def body(grad, owner, row_extent, col_extent, left_old, right_old, left_root, right_root):
@@ -265,7 +264,7 @@
     block_order = row_share * fsdp_count
     lanes = wire_lanes(row_share, col_share)
     wire = pltpu.VMEM((fsdp_count, wire_halves, lanes), bf16)
-    slots = pltpu.VMEM((lanes // lane_count, fsdp_count * wire_halves, lane_count), f32)
+    slots = pltpu.VMEM((lanes // lane_count, fsdp_count * wire_halves + 8, lane_count), f32)
     owner_row, live_rows, live_cols = owner[None, :], row_extent[None, :], col_extent[None, :]
     turned_grad = grad.transpose(1, 0, 2)
 
@@ -291,12 +290,13 @@
 
     root_shape = (block_order, block_order)
     half = rounded_up(col_share, 16)
+    held_rows = rounded_up(col_share, 8)
     left_high, left_low, right_pieces = call(
         functools.partial(prepare_kernel, row_share),
         [
             jax.ShapeDtypeStruct(root_shape, bf16),
             pltpu.HBM(root_shape, bf16),
-            jax.ShapeDtypeStruct((replica_count, 2 * half, col_share), bf16),
+            jax.ShapeDtypeStruct((2 * half, replica_count * held_rows), bf16),
         ],
         [vmem, vmem],
         "prepare",
@@ -306,16 +306,16 @@
     )(left_root[0], right_root[0])
 
     columns = call(
-        functools.partial(turn_kernel, row_share),
-        jax.ShapeDtypeStruct((col_share, block_order), bf16),
+        functools.partial(turn_kernel, row_share, col_share),
+        jax.ShapeDtypeStruct((held_rows, block_order), bf16),
         [vmem] * 4,
         "turn",
         2**20,
         [slots],
     )(owner_row, live_rows, live_cols, received)
-    block = lax.all_gather(columns, "replica", axis=0)
+    block = lax.all_gather(columns, "replica", axis=0, tiled=True)
     result = call(
-        functools.partial(update_kernel, row_share),
+        functools.partial(update_kernel, row_share, col_share),
         wire,
         [vmem] * 6 + [hbm],
         "update",
@@ -334,7 +334,7 @@
 
     stat = jax.ShapeDtypeStruct((col_share, block_order), f32)
     left_rows, right_rows = call(
-        functools.partial(stats_kernel, row_share),
+        functools.partial(stats_kernel, row_share, col_share),
         [stat, stat],
         [vmem, vmem, hbm],
         "stats",

time: 91.7 us -> 91.7 us (level)
  Pallas kernels: 14.2 us -> 12.5 us
  waiting for transfers between devices: 17.7 us -> 19.2 us
    pallas_call x3, Pallas kernels: 7.65 us -> 5.26 us  [the longest x1 2.83 us: body(): call(functools.partial(update_kernel, row_share, col_share), wire, [vmem]...]
    all_to_all x2, waiting for transfers between devices: 17.7 us -> 19.2 us  [exchange(): return lax.all_to_all(sent, 'fsdp', split_axis=0, concat_axis=0, tiled=True)]
  transfers between devices with their start and end apart: 2 -> 2, of which waited for: 2 -> 2; matrix products, arithmetic and copies ran while one was open for 3% -> 3% of each run, Pallas kernels for 9% -> 7%
where the time goes in v6:
time: 91.7 us; the launch traced here: 91.3 us
  starting transfers between devices  31.2 us (34%)
  blocking collectives  23 us (25%)
  waiting for transfers between devices  19.2 us (21%)
  Pallas kernels  12.5 us (14%)
  local copies, waits for them, and re-layouts  4.5 us (5%)
    all_to_all x2, starting transfers between devices, exchange(): return lax.all_to_all(sent, 'fsdp', split_axis=0, concat_axis=0, tiled=True)  31.2 us
    all_gather x1, blocking collectives, body(): block = lax.all_gather(columns, 'replica', axis=0, tiled=True)  23 us
    all_to_all x2, waiting for transfers between devices, exchange(): return lax.all_to_all(sent, 'fsdp', split_axis=0, concat_axis=0, tiled=True)  19.2 us
    unnamed x15, local copies, waits for them, and re-layouts  4.5 us
    pallas_call x1, Pallas kernels, body(): call(functools.partial(prepare_kernel, row_share), [jax.ShapeDtypeStruct(...  4.34 us
    pallas_call x1, Pallas kernels, body(): call(functools.partial(update_kernel, row_share, col_share), wire, [vmem]...  2.83 us
    pallas_call x1, Pallas kernels, body(): call(functools.partial(stats_kernel, row_share, col_share), [stat, stat],...  2.13 us
    pallas_call x1, Pallas kernels, body(): call(pack_kernel, wire, [hbm, hbm], 'pack', 2 ** 20, [pltpu.VMEM(owner_ro...  1.92 us
  transfers between devices with their start and end apart: 2, of which 2 were waited for; matrix products, arithmetic and copies ran while one was open for 3% of the time, Pallas kernels for 7%

profile of v6, /device:TPU:1, one launch (start us, length us, event | category | flops | bytes accessed | tf_op | source)
XLA Modules:
  0.0 91.3 jit_solution(17141426009081513589)
XLA Ops:
  0.6 1.9 %pack.1 = bf16[96,2,384]{2,1,0:T(2,128)(2,1)} custom-call(s32[1,72]{1,0:T(1,128)} %bitcast.14, bf16[7,72,84]{2,1,0:T(8,128)(2,1)} %bitcast.23), custom_call_target="tpu_custom_call" | custom-call | flops 1048576 | bytes 1048576 | tf_op jit(solution)/shard_map/pack/pallas_call | solution.py:275
  2.6 20.0 %all-to-all-start = ((bf16[96,2,384]{2,1,0:T(2,128)(2,1)}), bf16[96,2,384]{2,1,0:T(2,128)(2,1)S(1)}, u32[]{:S(2)}, u32[]{:S(2)}) async-start(bf16[96,2,384]{2,1,0:T(2,128)(2,1)} %pack.1), calls=%async_computation | async-start | bytes 294912 | tf_op jit(solution)/shard_map/all_to_all | solution.py:272
  22.6 1.0 %copy.23 = f32[1,84,672]{2,1,0:T(8,128)S(1)} copy(f32[1,84,672]{2,0,1:T(1,128)} %param.15) | data formatting | bytes 451584
  23.6 0.0 copy-start.3
  23.6 1.6 %copy-done.3 = f32[1,672,672]{2,1,0:T(8,128)S(1)} copy-done((f32[1,672,672]{2,1,0:T(8,128)S(1)}, f32[1,672,672]{2,1,0:T(8,128)}, u32[]{:S(2)}) %copy-start.3) | copy-done | bytes 1806360
  25.2 0.0 copy-start
  25.2 0.0 copy-start.1
  25.2 0.0 copy-start.2
  25.2 4.3 %prepare.1 = (bf16[672,672]{1,0:T(8,128)(2,1)S(1)}, bf16[672,672]{1,0:T(8,128)(2,1)}, bf16[192,704]{1,0:T(8,128)(2,1)S(1)}) custom-call(f32[672,672]{1,0:T(8,128)S(1)} %bitcast.22, f32[84,672]{1,0:T(8,128)S(1)} %bitcast.13), custom_call_target="tpu_custom_call" | custom-call | flops 2147483648 | bytes 1048576 | tf_op jit(solution)/shard_map/prepare/pallas_call | solution.py:294
  29.5 8.1 %all-to-all-done.wire_ref = bf16[96,2,384]{2,1,0:T(2,128)(2,1)S(1)} async-done(((bf16[96,2,384]{2,1,0:T(2,128)(2,1)}), bf16[96,2,384]{2,1,0:T(2,128)(2,1)S(1)}, u32[]{:S(2)}, u32[]{:S(2)}) %all-to-all-start) | async-done | bytes 147488 | tf_op jit(solution)/shard_map/all_to_all | solution.py:272
  37.7 0.0 copy-done
  37.7 0.0 copy-done.1
  37.7 0.0 copy-done.2
  37.7 0.3 turn.1.columns_ref
  38.0 23.0 %all_gather.3.block_ref = bf16[704,672]{1,0:T(8,128)(2,1)S(1)} all-gather(bf16[88,672]{1,0:T(8,128)(2,1)S(1)} %turn.1.columns_ref), channel_id=1, replica_groups=mesh['replica'=8,'fsdp'=96] {'replica'}, dimensions={0}, use_global_device_ids=true | all-gather | bytes 1064448 | tf_op jit(solution)/shard_map/all_gather | solution.py:316
  61.0 2.8 %update.1.after_ref = bf16[96,2,384]{2,1,0:T(2,128)(2,1)} custom-call(s32[1,72]{1,0:T(1,128)S(1)} %bitcast.16, s32[1,72]{1,0:T(1,128)S(1)} %bitcast.19, s32[1,72]{1,0:T(1,128)S(1)} %bitcast.21, bf16[704,672]{1,0:T(8,128)(2,1)S(1)} %all_gather.3.block_ref, bf16[192,704]{1,0:T(8,128)(2,1)S(1)} %get-tuple-element.8.right_ref, ...), custom_call_target="tpu_custom_call" | custom-call | flops 1073741824 | bytes 1048576 | tf_op jit(solution)/shard_map/update/pallas_call | solution.py:317
  63.8 0.0 copy-start.4
  63.9 0.0 copy-start.5
  63.9 11.1 %all-to-all-start.1 = ((bf16[96,2,384]{2,1,0:T(2,128)(2,1)}), bf16[96,2,384]{2,1,0:T(2,128)(2,1)S(1)}, u32[]{:S(2)}, u32[]{:S(2)}) async-start(bf16[96,2,384]{2,1,0:T(2,128)(2,1)} %update.1.after_ref), calls=%async_computation.1 | async-start | bytes 294912 | tf_op jit(solution)/shard_map/all_to_all | solution.py:272
  75.0 2.1 %stats.1 = (f32[84,672]{1,0:T(8,128)S(1)}, f32[84,672]{1,0:T(8,128)S(1)}) custom-call(bf16[704,672]{1,0:T(8,128)(2,1)S(1)} %all_gather.3.block_ref, bf16[88,672]{1,0:T(8,128)(2,1)S(1)} %turn.1.columns_ref, bf16[96,2,384]{2,1,0:T(2,128)(2,1)} %update.1.after_ref), custom_call_target="tpu_custom_call" | custom-call | flops 536870912 | bytes 1048576 | tf_op jit(solution)/shard_map/stats/pallas_call | solution.py:336
  77.1 0.0 copy-done.4
  77.2 0.0 copy-done.5
  77.2 0.1 bitcast_add_fusion
  77.3 1.0 %copy.14 = f32[1,84,672]{2,0,1:T(1,128)} copy(f32[1,84,672]{2,1,0:T(8,128)S(1)} %get-tuple-element.16) | data formatting | bytes 451584
  78.2 1.0 %copy.13 = f32[1,84,672]{2,0,1:T(1,128)} copy(f32[1,84,672]{2,1,0:T(8,128)S(1)} %get-tuple-element.17) | data formatting | bytes 451584
  79.2 11.1 %all-to-all-done.1.wire_ref = bf16[96,2,384]{2,1,0:T(2,128)(2,1)S(1)} async-done(((bf16[96,2,384]{2,1,0:T(2,128)(2,1)}), bf16[96,2,384]{2,1,0:T(2,128)(2,1)S(1)}, u32[]{:S(2)}, u32[]{:S(2)}) %all-to-all-start.1) | async-done | bytes 147488 | tf_op jit(solution)/shard_map/all_to_all | solution.py:272
  90.3 1.0 %unpack.1 = bf16[7,72,84]{2,1,0:T(8,128)(2,1)} custom-call(s32[1,72]{1,0:T(1,128)S(1)} %bitcast.17, bf16[96,2,384]{2,1,0:T(2,128)(2,1)S(1)} %all-to-all-done.1.wire_ref), custom_call_target="tpu_custom_call" | custom-call | flops 1048576 | bytes 1048576 | tf_op jit(solution)/shard_map/unpack/pallas_call | solution.py:346
Async XLA Ops:
  2.6 35.1 %all-to-all-start = ((bf16[96,2,384]{2,1,0:T(2,128)(2,1)}), bf16[96,2,384]{2,1,0:T(2,128)(2,1)S(1)}, u32[]{:S(2)}, u32[]{:S(2)}) async-start(bf16[96,2,384]{2,1,0:T(2,128)(2,1)} %pack.1), calls=%async_computation | async-start | bytes 294912 | tf_op jit(solution)/shard_map/all_to_all | solution.py:272
  23.6 1.6 %copy-start.3 = (f32[1,672,672]{2,1,0:T(8,128)S(1)}, f32[1,672,672]{2,1,0:T(8,128)}, u32[]{:S(2)}) copy-start(f32[1,672,672]{2,1,0:T(8,128)} %param.14) | copy-start | bytes 5419012
  25.2 12.5 %copy-start = (s32[72]{0:T(128)S(1)}, s32[72]{0:T(128)}, u32[]{:S(2)}) copy-start(s32[72]{0:T(128)} %param.9) | copy-start | bytes 868
  25.2 12.5 %copy-start.1 = (s32[72]{0:T(128)S(1)}, s32[72]{0:T(128)}, u32[]{:S(2)}) copy-start(s32[72]{0:T(128)} %param.10) | copy-start | bytes 868
  25.2 12.5 %copy-start.2 = (s32[72]{0:T(128)S(1)}, s32[72]{0:T(128)}, u32[]{:S(2)}) copy-start(s32[72]{0:T(128)} %param.11) | copy-start | bytes 868
  63.8 13.3 %copy-start.4 = (f32[1,84,672]{2,0,1:T(1,128)S(1)}, f32[1,84,672]{2,0,1:T(1,128)}, u32[]{:S(2)}) copy-start(f32[1,84,672]{2,0,1:T(1,128)} %param.13) | copy-start | bytes 677380
  63.9 13.3 %copy-start.5 = (f32[1,84,672]{2,0,1:T(1,128)S(1)}, f32[1,84,672]{2,0,1:T(1,128)}, u32[]{:S(2)}) copy-start(f32[1,84,672]{2,0,1:T(1,128)} %param.12) | copy-start | bytes 677380
  63.9 26.4 %all-to-all-start.1 = ((bf16[96,2,384]{2,1,0:T(2,128)(2,1)}), bf16[96,2,384]{2,1,0:T(2,128)(2,1)S(1)}, u32[]{:S(2)}, u32[]{:S(2)}) async-start(bf16[96,2,384]{2,1,0:T(2,128)(2,1)} %update.1.after_ref), calls=%async_computation.1 | async-start | bytes 294912 | tf_op jit(solution)/shard_map/all_to_all | solution.py:272

commit v7 on v6

--- a/solution.py
+++ b/solution.py
@@ -130,6 +130,18 @@
             update_ref[i] = picked[:, start : start + col_share].astype(bf16)
 
 
+def folded(columns, col_share):
+    quarter = col_share // 4
+    wide = columns.shape[1]
+    piece = wide // 3
+    rest = columns[3 * quarter : col_share]
+    rest = [rest[:, t * piece : (t + 1) * piece] for t in range(3)]
+    empty = rounded_up(3 * quarter, 16) - 3 * quarter
+    top = jnp.concatenate([columns[: 3 * quarter], jnp.zeros((empty, wide), f32)], axis=0)
+    rest = jnp.concatenate([*rest, jnp.zeros((empty, piece), f32)], axis=0)
+    return jnp.concatenate([top, rest], axis=1)
+
+
 def order_matrix(row_share, fsdp_count, forward):
     parts = []
     for i in range(row_share):
@@ -162,13 +174,28 @@
     replica_count = block_order // col_share
     right = right_ref[...]
     right_high = right.astype(bf16).astype(f32)
-    filler = jnp.zeros((pieces_ref.shape[0] // 2 - col_share, block_order), f32)
+    filler = jnp.zeros((pieces_ref.shape[0] // 8 - col_share, block_order), f32)
     both = jnp.concatenate([right_high, filler, right - right_high, filler], axis=0)
-    gap = jnp.zeros((both.shape[0], pieces_ref.shape[1] // replica_count - col_share), f32)
+    quarter = col_share // 4
+    held_rows = pieces_ref.shape[1] // replica_count
+
+    def blank(count):
+        return jnp.zeros((both.shape[0], count), f32)
+
     spaced = []
     for n in range(replica_count):
-        spaced += [both[:, n * col_share : (n + 1) * col_share], gap]
-    pieces_ref[...] = jnp.concatenate(spaced, axis=1).astype(bf16)
+        start = n * col_share
+        spaced += [both[:, start : start + 3 * quarter], blank(held_rows - 3 * quarter)]
+    pieces_ref[: both.shape[0]] = jnp.concatenate(spaced, axis=1).astype(bf16)
+    for t in range(3):
+        spaced = []
+        for n in range(replica_count):
+            start = n * col_share + 3 * quarter
+            if t:
+                spaced.append(blank(t * quarter))
+            spaced += [both[:, start : start + quarter], blank(held_rows - (t + 1) * quarter)]
+        held = slice((t + 1) * both.shape[0], (t + 2) * both.shape[0])
+        pieces_ref[held] = jnp.concatenate(spaced, axis=1).astype(bf16)
     copy.wait()
 
 
@@ -178,7 +205,7 @@
     return jnp.sum(values, axis=1, keepdims=True).astype(jnp.int32)
 
 
-def turn_kernel(row_share, col_share, owner_ref, rows_ref, cols_ref, wire_ref, columns_ref, slots):
+def turn_kernel(row_share, col_share, owner_ref, rows_ref, cols_ref, wire_ref, columns_ref, folded_ref, slots):
     held_rows = columns_ref.shape[0]
     fsdp_count = wire_ref.shape[0]
     per_half = per_half_of(row_share)
@@ -195,7 +222,9 @@
             start = (i - h * per_half) * pitch
             keep = col_live & (iota(shape, 1) * row_share + i < live_rows)
             pieces.append(jnp.where(keep, turned[start : start + held_rows], 0.0))
-    columns_ref[...] = jnp.concatenate(pieces, axis=1).astype(bf16)
+    columns = jnp.concatenate(pieces, axis=1)
+    columns_ref[...] = columns.astype(bf16)
+    folded_ref[...] = folded(columns, col_share).astype(bf16)
 
 
 def update_kernel(
@@ -204,15 +233,21 @@
 ):
     copy = pltpu.make_async_copy(left_low_hbm, left_low_ref, sem.at[0])
     copy.start()
-    block_order = block_ref.shape[1]
+    block_order = left_high_ref.shape[0]
     fsdp_count = block_order // row_share
     per_half = per_half_of(row_share)
     pitch = pitch_of(col_share)
-    half = right_ref.shape[0] // 2
+    half = right_ref.shape[0] // 8
     live_rows = owned_extent(owner_ref, rows_ref)
     live_cols = owned_extent(owner_ref, cols_ref) - lax.axis_index("replica") * col_share
-    total = jnp.dot(right_ref[...], block_ref[...], preferred_element_type=f32)
+    whole = block_order // lane_count * lane_count
+    rest = jnp.dot(right_ref[2 * half :], block_ref[:, whole:], preferred_element_type=f32)
+    rest = rest[:, block_order - whole :].reshape(3, 2, half, block_order // 3)
+    total = jnp.dot(
+        right_ref[: 2 * half], block_ref[:, :block_order], preferred_element_type=f32
+    )
     product = total[:half] + total[half:]
+    product += jnp.concatenate([rest[t, 0] + rest[t, 1] for t in range(3)], axis=1)
     product = jnp.concatenate(
         [product, jnp.zeros((lane_count - half, block_order), f32)], axis=0
     )
@@ -244,17 +279,39 @@
     rows_start = lax.axis_index("replica") * col_share
     shape = (block_order, col_share)
     mine = one_hot(iota(shape, 0) == iota(shape, 1) + rows_start)
-    natural = jnp.dot(block_ref[...], order, preferred_element_type=f32).astype(bf16)
+    replica_count = block_order // col_share
+    quarter = col_share // 4
+    piece = block_order // 3
+    held_rows = block_ref.shape[0] // replica_count
+    top = block_ref[:, :block_order]
+    rest = block_ref[:, block_order:]
+    columns = columns_ref[...]
+    last = (((1,), (1,)), ((), ()))
+    first = (((0,), (0,)), ((), ()))
+    with_top = lax.dot_general(columns, top, last, preferred_element_type=f32)
+    natural_rest, with_rest = [], []
+    for t in range(3):
+        held = slice(t * piece, (t + 1) * piece)
+        natural_rest.append(jnp.dot(rest, order[held], preferred_element_type=f32))
+        with_rest.append(
+            lax.dot_general(columns[:, held], rest, last, preferred_element_type=f32)
+        )
+    natural = jnp.dot(top, order, preferred_element_type=f32).astype(bf16)
     picked = jnp.dot(natural, mine, preferred_element_type=f32).astype(bf16)
-    left_ref[...] = lax.dot_general(
-        picked, natural, (((0,), (0,)), ((), ())), preferred_element_type=f32
-    )
-    right = lax.dot_general(
-        columns_ref[...], block_ref[...], (((1,), (1,)), ((), ())), preferred_element_type=f32
-    )[:col_share]
-    for n in range(block_order // col_share):
-        held = right[:, n * held_rows : n * held_rows + col_share]
-        right_ref[:, n * col_share : (n + 1) * col_share] = held
+    left = lax.dot_general(picked, natural, first, preferred_element_type=f32)
+    for n in range(replica_count):
+        held = [n * held_rows + t * quarter for t in range(3)]
+        natural = sum(natural_rest[t][held[t] : held[t] + quarter] for t in range(3)).astype(bf16)
+        picked = jnp.dot(natural, mine, preferred_element_type=f32).astype(bf16)
+        left += lax.dot_general(picked, natural, first, preferred_element_type=f32)
+        start = n * col_share
+        right_ref[:, start : start + 3 * quarter] = with_top[
+            :col_share, n * held_rows : n * held_rows + 3 * quarter
+        ]
+        right_ref[:, start + 3 * quarter : start + col_share] = sum(
+            with_rest[t][:col_share, held[t] : held[t] + quarter] for t in range(3)
+        )
+    left_ref[...] = left
 
 
 def body(grad, owner, row_extent, col_extent, left_old, right_old, left_root, right_root):
@@ -291,12 +348,13 @@
     root_shape = (block_order, block_order)
     half = rounded_up(col_share, 16)
     held_rows = rounded_up(col_share, 8)
+    folded_shape = (rounded_up(col_share // 4 * 3, 16), block_order // 3 * 4)
     left_high, left_low, right_pieces = call(
         functools.partial(prepare_kernel, row_share),
         [
             jax.ShapeDtypeStruct(root_shape, bf16),
             pltpu.HBM(root_shape, bf16),
-            jax.ShapeDtypeStruct((2 * half, replica_count * held_rows), bf16),
+            jax.ShapeDtypeStruct((8 * half, replica_count * folded_shape[0]), bf16),
         ],
         [vmem, vmem],
         "prepare",
@@ -305,15 +363,18 @@
         [vmem, hbm, vmem],
     )(left_root[0], right_root[0])
 
-    columns = call(
+    columns, sent = call(
         functools.partial(turn_kernel, row_share, col_share),
-        jax.ShapeDtypeStruct((held_rows, block_order), bf16),
+        [
+            jax.ShapeDtypeStruct((held_rows, block_order), bf16),
+            jax.ShapeDtypeStruct(folded_shape, bf16),
+        ],
         [vmem] * 4,
         "turn",
         2**20,
         [slots],
     )(owner_row, live_rows, live_cols, received)
-    block = lax.all_gather(columns, "replica", axis=0, tiled=True)
+    block = lax.all_gather(sent, "replica", axis=0, tiled=True)
     result = call(
         functools.partial(update_kernel, row_share, col_share),
         wire,

time: 91.7 us -> 91.5 us (level)
  Pallas kernels: 12.5 us -> 14.9 us
  waiting for transfers between devices: 19.2 us -> 17.1 us
    pallas_call x1, Pallas kernels: 2.13 us -> 4.37 us  [body(): call(functools.partial(stats_kernel, row_share, col_share), [stat, stat],...]
    all_to_all x2, waiting for transfers between devices: 19.2 us -> 17.1 us  [exchange(): return lax.all_to_all(sent, 'fsdp', split_axis=0, concat_axis=0, tiled=True)]
  transfers between devices with their start and end apart: 2 -> 2, of which waited for: 2 -> 2; matrix products, arithmetic and copies ran while one was open for 3% -> 3% of each run, Pallas kernels for 7% -> 9%
where the time goes in v7:
time: 91.5 us; the launch traced here: 91.2 us
  starting transfers between devices  31 us (34%)
  blocking collectives  22.8 us (25%)
  waiting for transfers between devices  17.1 us (19%)
  Pallas kernels  14.9 us (16%)
  local copies, waits for them, and re-layouts  4.5 us (5%)
    all_to_all x2, starting transfers between devices, exchange(): return lax.all_to_all(sent, 'fsdp', split_axis=0, concat_axis=0, tiled=True)  31 us
    all_gather x1, blocking collectives, body(): block = lax.all_gather(sent, 'replica', axis=0, tiled=True)  22.8 us
    all_to_all x2, waiting for transfers between devices, exchange(): return lax.all_to_all(sent, 'fsdp', split_axis=0, concat_axis=0, tiled=True)  17.1 us
    unnamed x15, local copies, waits for them, and re-layouts  4.5 us
    pallas_call x1, Pallas kernels, body(): call(functools.partial(stats_kernel, row_share, col_share), [stat, stat],...  4.37 us
    pallas_call x1, Pallas kernels, body(): call(functools.partial(prepare_kernel, row_share), [jax.ShapeDtypeStruct(...  4.26 us
    pallas_call x1, Pallas kernels, body(): call(functools.partial(update_kernel, row_share, col_share), wire, [vmem]...  2.91 us
    pallas_call x1, Pallas kernels, body(): call(pack_kernel, wire, [hbm, hbm], 'pack', 2 ** 20, [pltpu.VMEM(owner_ro...  1.92 us
  transfers between devices with their start and end apart: 2, of which 2 were waited for; matrix products, arithmetic and copies ran while one was open for 3% of the time, Pallas kernels for 9%

profile of v7, /device:TPU:1, one launch (start us, length us, event | category | flops | bytes accessed | tf_op | source)
XLA Modules:
  0.0 91.2 jit_solution(7497905128539912004)
XLA Ops:
  0.6 1.9 %pack.1 = bf16[96,2,384]{2,1,0:T(2,128)(2,1)} custom-call(s32[1,72]{1,0:T(1,128)} %bitcast.14, bf16[7,72,84]{2,1,0:T(8,128)(2,1)} %bitcast.23), custom_call_target="tpu_custom_call" | custom-call | flops 1048576 | bytes 1048576 | tf_op jit(solution)/shard_map/pack/pallas_call | solution.py:332
  2.6 20.0 %all-to-all-start = ((bf16[96,2,384]{2,1,0:T(2,128)(2,1)}), bf16[96,2,384]{2,1,0:T(2,128)(2,1)S(1)}, u32[]{:S(2)}, u32[]{:S(2)}) async-start(bf16[96,2,384]{2,1,0:T(2,128)(2,1)} %pack.1), calls=%async_computation | async-start | bytes 294912 | tf_op jit(solution)/shard_map/all_to_all | solution.py:329
  22.6 1.0 %copy.23 = f32[1,84,672]{2,1,0:T(8,128)S(1)} copy(f32[1,84,672]{2,0,1:T(1,128)} %param.15) | data formatting | bytes 451584
  23.6 0.0 copy-start.3
  23.6 1.6 %copy-done.3 = f32[1,672,672]{2,1,0:T(8,128)S(1)} copy-done((f32[1,672,672]{2,1,0:T(8,128)S(1)}, f32[1,672,672]{2,1,0:T(8,128)}, u32[]{:S(2)}) %copy-start.3) | copy-done | bytes 1806360
  25.2 0.0 copy-start
  25.2 0.0 copy-start.1
  25.2 0.0 copy-start.2
  25.2 4.3 %prepare.1 = (bf16[672,672]{1,0:T(8,128)(2,1)S(1)}, bf16[672,672]{1,0:T(8,128)(2,1)}, bf16[768,512]{1,0:T(8,128)(2,1)S(1)}) custom-call(f32[672,672]{1,0:T(8,128)S(1)} %bitcast.22, f32[84,672]{1,0:T(8,128)S(1)} %bitcast.13), custom_call_target="tpu_custom_call" | custom-call | flops 2147483648 | bytes 1048576 | tf_op jit(solution)/shard_map/prepare/pallas_call | solution.py:352
  29.4 8.2 %all-to-all-done.wire_ref = bf16[96,2,384]{2,1,0:T(2,128)(2,1)S(1)} async-done(((bf16[96,2,384]{2,1,0:T(2,128)(2,1)}), bf16[96,2,384]{2,1,0:T(2,128)(2,1)S(1)}, u32[]{:S(2)}, u32[]{:S(2)}) %all-to-all-start) | async-done | bytes 147488 | tf_op jit(solution)/shard_map/all_to_all | solution.py:329
  37.7 0.0 copy-done
  37.7 0.0 copy-done.1
  37.7 0.0 copy-done.2
  37.7 0.4 turn.1
  38.1 22.8 %all_gather.3.block_ref = bf16[512,896]{1,0:T(8,128)(2,1)S(1)} all-gather(bf16[64,896]{1,0:T(8,128)(2,1)S(1)} %get-tuple-element.10), channel_id=1, replica_groups=mesh['replica'=8,'fsdp'=96] {'replica'}, dimensions={0}, use_global_device_ids=true | all-gather | bytes 1032192 | tf_op jit(solution)/shard_map/all_gather | solution.py:377
  60.9 2.9 %update.1.after_ref = bf16[96,2,384]{2,1,0:T(2,128)(2,1)} custom-call(s32[1,72]{1,0:T(1,128)S(1)} %bitcast.16, s32[1,72]{1,0:T(1,128)S(1)} %bitcast.19, s32[1,72]{1,0:T(1,128)S(1)} %bitcast.21, bf16[512,896]{1,0:T(8,128)(2,1)S(1)} %all_gather.3.block_ref, bf16[768,512]{1,0:T(8,128)(2,1)S(1)} %get-tuple-element.11.right_ref, ...), custom_call_target="tpu_custom_call" | custom-call | flops 1073741824 | bytes 1048576 | tf_op jit(solution)/shard_map/update/pallas_call | solution.py:378
  63.8 0.0 copy-start.4
  63.8 0.0 copy-start.5
  63.9 11.0 %all-to-all-start.1 = ((bf16[96,2,384]{2,1,0:T(2,128)(2,1)}), bf16[96,2,384]{2,1,0:T(2,128)(2,1)S(1)}, u32[]{:S(2)}, u32[]{:S(2)}) async-start(bf16[96,2,384]{2,1,0:T(2,128)(2,1)} %update.1.after_ref), calls=%async_computation.1 | async-start | bytes 294912 | tf_op jit(solution)/shard_map/all_to_all | solution.py:329
  74.9 4.4 %stats.1 = (f32[84,672]{1,0:T(8,128)S(1)}, f32[84,672]{1,0:T(8,128)S(1)}) custom-call(bf16[512,896]{1,0:T(8,128)(2,1)S(1)} %all_gather.3.block_ref, bf16[88,672]{1,0:T(8,128)(2,1)S(1)} %get-tuple-element.14.columns_ref, bf16[96,2,384]{2,1,0:T(2,128)(2,1)} %update.1.after_ref), custom_call_target="tpu_custom_call" | custom-call | flops 536870912 | bytes 1048576 | tf_op jit(solution)/shard_map/stats/pallas_call | solution.py:397
  79.2 0.0 copy-done.4
  79.3 0.0 copy-done.5
  79.3 0.1 bitcast_add_fusion
  79.4 1.0 %copy.14 = f32[1,84,672]{2,0,1:T(1,128)} copy(f32[1,84,672]{2,1,0:T(8,128)S(1)} %get-tuple-element.20) | data formatting | bytes 451584
  80.3 1.0 %copy.13 = f32[1,84,672]{2,0,1:T(1,128)} copy(f32[1,84,672]{2,1,0:T(8,128)S(1)} %get-tuple-element.21) | data formatting | bytes 451584
  81.3 8.9 %all-to-all-done.1.wire_ref = bf16[96,2,384]{2,1,0:T(2,128)(2,1)S(1)} async-done(((bf16[96,2,384]{2,1,0:T(2,128)(2,1)}), bf16[96,2,384]{2,1,0:T(2,128)(2,1)S(1)}, u32[]{:S(2)}, u32[]{:S(2)}) %all-to-all-start.1) | async-done | bytes 147488 | tf_op jit(solution)/shard_map/all_to_all | solution.py:329
  90.2 1.0 %unpack.1 = bf16[7,72,84]{2,1,0:T(8,128)(2,1)} custom-call(s32[1,72]{1,0:T(1,128)S(1)} %bitcast.17, bf16[96,2,384]{2,1,0:T(2,128)(2,1)S(1)} %all-to-all-done.1.wire_ref), custom_call_target="tpu_custom_call" | custom-call | flops 1048576 | bytes 1048576 | tf_op jit(solution)/shard_map/unpack/pallas_call | solution.py:407
Async XLA Ops:
  2.6 35.1 %all-to-all-start = ((bf16[96,2,384]{2,1,0:T(2,128)(2,1)}), bf16[96,2,384]{2,1,0:T(2,128)(2,1)S(1)}, u32[]{:S(2)}, u32[]{:S(2)}) async-start(bf16[96,2,384]{2,1,0:T(2,128)(2,1)} %pack.1), calls=%async_computation | async-start | bytes 294912 | tf_op jit(solution)/shard_map/all_to_all | solution.py:329
  23.6 1.6 %copy-start.3 = (f32[1,672,672]{2,1,0:T(8,128)S(1)}, f32[1,672,672]{2,1,0:T(8,128)}, u32[]{:S(2)}) copy-start(f32[1,672,672]{2,1,0:T(8,128)} %param.14) | copy-start | bytes 5419012
  25.2 12.5 %copy-start = (s32[72]{0:T(128)S(1)}, s32[72]{0:T(128)}, u32[]{:S(2)}) copy-start(s32[72]{0:T(128)} %param.9) | copy-start | bytes 868
  25.2 12.5 %copy-start.1 = (s32[72]{0:T(128)S(1)}, s32[72]{0:T(128)}, u32[]{:S(2)}) copy-start(s32[72]{0:T(128)} %param.10) | copy-start | bytes 868
  25.2 12.5 %copy-start.2 = (s32[72]{0:T(128)S(1)}, s32[72]{0:T(128)}, u32[]{:S(2)}) copy-start(s32[72]{0:T(128)} %param.11) | copy-start | bytes 868
  63.8 15.4 %copy-start.4 = (f32[1,84,672]{2,0,1:T(1,128)S(1)}, f32[1,84,672]{2,0,1:T(1,128)}, u32[]{:S(2)}) copy-start(f32[1,84,672]{2,0,1:T(1,128)} %param.13) | copy-start | bytes 677380
  63.8 15.4 %copy-start.5 = (f32[1,84,672]{2,0,1:T(1,128)S(1)}, f32[1,84,672]{2,0,1:T(1,128)}, u32[]{:S(2)}) copy-start(f32[1,84,672]{2,0,1:T(1,128)} %param.12) | copy-start | bytes 677380
  63.9 26.3 %all-to-all-start.1 = ((bf16[96,2,384]{2,1,0:T(2,128)(2,1)}), bf16[96,2,384]{2,1,0:T(2,128)(2,1)S(1)}, u32[]{:S(2)}, u32[]{:S(2)}) async-start(bf16[96,2,384]{2,1,0:T(2,128)(2,1)} %update.1.after_ref), calls=%async_computation.1 | async-start | bytes 294912 | tf_op jit(solution)/shard_map/all_to_all | solution.py:329

commit v8 on v7

--- a/solution.py
+++ b/solution.py
@@ -10,6 +10,7 @@
 decay_rate = 0.9
 lane_count = 128
 wire_halves = 2
+send_parts = 2
 f32 = jnp.float32
 bf16 = jnp.bfloat16
 vmem = pl.BlockSpec(memory_space=pltpu.VMEM)
@@ -154,12 +155,22 @@
     return jnp.concatenate(parts, axis=0 if forward else 1)
 
 
+def wire_order_matrix(row_share, fsdp_count):
+    count = fsdp_count // send_parts
+    shape = (count, row_share * fsdp_count)
+    parts = []
+    for q in range(send_parts):
+        for i in range(row_share):
+            parts.append(one_hot((iota(shape, 0) + q * count) * row_share + i == iota(shape, 1)))
+    return jnp.concatenate(parts, axis=0)
+
+
 def prepare_kernel(
     row_share, left_ref, right_ref, left_high_ref, left_low_hbm, pieces_ref, left_low_ref, sem
 ):
     block_order = left_ref.shape[0]
     fsdp_count = block_order // row_share
-    rows = order_matrix(row_share, fsdp_count, True)
+    rows = wire_order_matrix(row_share, fsdp_count)
     cols = order_matrix(row_share, fsdp_count, False)
     left = left_ref[...]
     left_high = left.astype(bf16)
@@ -229,7 +240,7 @@
 
 def update_kernel(
     row_share, col_share, owner_ref, rows_ref, cols_ref, block_ref, right_ref, left_high_ref,
-    left_low_hbm, wire_ref, slots, left_low_ref, sem,
+    left_low_hbm, wire_hbm, slots, wire_ref, left_low_ref, sem,
 ):
     copy = pltpu.make_async_copy(left_low_hbm, left_low_ref, sem.at[0])
     copy.start()
@@ -258,19 +269,38 @@
         left_high_ref[...], jnp.concatenate([high, low], axis=0), last, preferred_element_type=f32
     )
     copy.wait()
-    second = lax.dot_general(left_low_ref[...], high, last, preferred_element_type=f32)
-    result = first[:, :lane_count] + first[:, lane_count:] + second
-    shape = (fsdp_count, lane_count)
+    count = fsdp_count // send_parts
+    shape = (count, lane_count)
     lane = iota(shape, 1)
     col_live = (lane < live_cols) & (lane < col_share)
-    for h in range(wire_halves):
-        pieces = []
-        for i in range(h * per_half, min(row_share, (h + 1) * per_half)):
-            keep = col_live & (iota(shape, 0) * row_share + i < live_rows)
-            piece = jnp.where(keep, result[i * fsdp_count : (i + 1) * fsdp_count], 0.0)
-            pieces.append(piece[:, :pitch])
-        put_half(slots, h, joined(pieces, wire_ref.shape[2]))
-    to_wire(slots, wire_ref)
+    sends = []
+    for q in range(send_parts):
+        held = slice(q * row_share * count, (q + 1) * row_share * count)
+        second = lax.dot_general(left_low_ref[held], high, last, preferred_element_type=f32)
+        result = first[held, :lane_count] + first[held, lane_count:] + second
+        for h in range(wire_halves):
+            pieces = []
+            for i in range(h * per_half, min(row_share, (h + 1) * per_half)):
+                keep = col_live & ((iota(shape, 0) + q * count) * row_share + i < live_rows)
+                piece = jnp.where(keep, result[i * count : (i + 1) * count], 0.0)
+                pieces.append(piece[:, :pitch])
+            value = joined(pieces, wire_ref.shape[2])
+            for t, part in enumerate(tiles(value.shape[1])):
+                place = pl.ds(q * count * wire_halves + h, count, stride=wire_halves)
+                slots[t, place, :] = value[:, part]
+        owners = slice(q * count, (q + 1) * count)
+        for t, part in enumerate(tiles(wire_ref.shape[2])):
+            rows = slots[t, q * count * wire_halves : (q + 1) * count * wire_halves].astype(bf16)
+            wire_ref[owners, :, part] = rows.reshape(count, wire_halves, lane_count)
+        send = pltpu.make_async_copy(
+            wire_ref.at[pl.ds(q * count, count)],
+            wire_hbm.at[pl.ds(q * count, count)],
+            sem.at[1 + q],
+        )
+        send.start()
+        sends.append(send)
+    for send in sends:
+        send.wait()
 
 
 def stats_kernel(row_share, col_share, block_ref, columns_ref, after_ref, left_ref, right_ref):
@@ -377,11 +407,12 @@
     block = lax.all_gather(sent, "replica", axis=0, tiled=True)
     result = call(
         functools.partial(update_kernel, row_share, col_share),
-        wire,
+        pltpu.HBM(wire.shape, bf16),
         [vmem] * 6 + [hbm],
         "update",
         2**30,
-        [slots, pltpu.VMEM(root_shape, bf16), pltpu.SemaphoreType.DMA((1,))],
+        [slots, wire, pltpu.VMEM(root_shape, bf16), pltpu.SemaphoreType.DMA((1 + send_parts,))],
+        hbm,
     )(
         owner_row,
         live_rows,

time: 91.5 us -> 91.4 us (level)
  waiting for transfers between devices: 17.1 us -> 16.1 us
  local copies, waits for them, and re-layouts: 4.5 us -> 5.43 us
    unnamed x15 -> x17, local copies, waits for them, and re-layouts: 4.5 us -> 5.43 us
    all_to_all x2, waiting for transfers between devices: 17.1 us -> 16.1 us  [exchange(): return lax.all_to_all(sent, 'fsdp', split_axis=0, concat_axis=0, tiled=True)]
where the time goes in v8:
time: 91.4 us; the launch traced here: 91 us
  starting transfers between devices  31 us (34%)
  blocking collectives  22.8 us (25%)
  waiting for transfers between devices  16.1 us (18%)
  Pallas kernels  14.7 us (16%)
  local copies, waits for them, and re-layouts  5.43 us (6%)
    all_to_all x2, starting transfers between devices, exchange(): return lax.all_to_all(sent, 'fsdp', split_axis=0, concat_axis=0, tiled=True)  31 us
    all_gather x1, blocking collectives, body(): block = lax.all_gather(sent, 'replica', axis=0, tiled=True)  22.8 us
    all_to_all x2, waiting for transfers between devices, exchange(): return lax.all_to_all(sent, 'fsdp', split_axis=0, concat_axis=0, tiled=True)  16.1 us
    unnamed x17, local copies, waits for them, and re-layouts  5.43 us
    pallas_call x1, Pallas kernels, body(): call(functools.partial(stats_kernel, row_share, col_share), [stat, stat],...  4.37 us
    pallas_call x1, Pallas kernels, body(): call(functools.partial(prepare_kernel, row_share), [jax.ShapeDtypeStruct(...  4.24 us
    pallas_call x1, Pallas kernels, body(): call(functools.partial(update_kernel, row_share, col_share), pltpu.HBM(wi...  2.74 us
    pallas_call x1, Pallas kernels, body(): call(pack_kernel, wire, [hbm, hbm], 'pack', 2 ** 20, [pltpu.VMEM(owner_ro...  1.92 us
  transfers between devices with their start and end apart: 2, of which 2 were waited for; matrix products, arithmetic and copies ran while one was open for 3% of the time, Pallas kernels for 9%

profile of v8, /device:TPU:1, one launch (start us, length us, event | category | flops | bytes accessed | tf_op | source)
XLA Modules:
  0.0 91.0 jit_solution(8153422694571179976)
XLA Ops:
  0.6 1.9 %pack.1 = bf16[96,2,384]{2,1,0:T(2,128)(2,1)} custom-call(s32[1,72]{1,0:T(1,128)} %bitcast.14, bf16[7,72,84]{2,1,0:T(8,128)(2,1)} %bitcast.23), custom_call_target="tpu_custom_call" | custom-call | flops 1048576 | bytes 1048576 | tf_op jit(solution)/shard_map/pack/pallas_call | solution.py:362
  2.6 20.0 %all-to-all-start = ((bf16[96,2,384]{2,1,0:T(2,128)(2,1)}), bf16[96,2,384]{2,1,0:T(2,128)(2,1)S(1)}, u32[]{:S(2)}, u32[]{:S(2)}) async-start(bf16[96,2,384]{2,1,0:T(2,128)(2,1)} %pack.1), calls=%async_computation | async-start | bytes 294912 | tf_op jit(solution)/shard_map/all_to_all | solution.py:359
  22.6 1.0 %copy.23 = f32[1,84,672]{2,1,0:T(8,128)S(1)} copy(f32[1,84,672]{2,0,1:T(1,128)} %param.15) | data formatting | bytes 451584
  23.6 0.0 copy-start.4
  23.6 1.6 %copy-done.4 = f32[1,672,672]{2,1,0:T(8,128)S(1)} copy-done((f32[1,672,672]{2,1,0:T(8,128)S(1)}, f32[1,672,672]{2,1,0:T(8,128)}, u32[]{:S(2)}) %copy-start.4) | copy-done | bytes 1806360
  25.2 0.0 copy-start.1
  25.2 0.0 copy-start.2
  25.2 0.0 copy-start.3
  25.2 4.2 %prepare.1 = (bf16[672,672]{1,0:T(8,128)(2,1)S(1)}, bf16[672,672]{1,0:T(8,128)(2,1)}, bf16[768,512]{1,0:T(8,128)(2,1)S(1)}) custom-call(f32[672,672]{1,0:T(8,128)S(1)} %bitcast.22, f32[84,672]{1,0:T(8,128)S(1)} %bitcast.13), custom_call_target="tpu_custom_call" | custom-call | flops 2147483648 | bytes 1048576 | tf_op jit(solution)/shard_map/prepare/pallas_call | solution.py:382
  29.4 8.2 %all-to-all-done.wire_ref = bf16[96,2,384]{2,1,0:T(2,128)(2,1)S(1)} async-done(((bf16[96,2,384]{2,1,0:T(2,128)(2,1)}), bf16[96,2,384]{2,1,0:T(2,128)(2,1)S(1)}, u32[]{:S(2)}, u32[]{:S(2)}) %all-to-all-start) | async-done | bytes 147488 | tf_op jit(solution)/shard_map/all_to_all | solution.py:359
  37.7 0.0 copy-done.1
  37.7 0.0 copy-done.2
  37.7 0.0 copy-done.3
  37.7 0.4 turn.1
  38.1 22.8 %all_gather.3.block_ref = bf16[512,896]{1,0:T(8,128)(2,1)S(1)} all-gather(bf16[64,896]{1,0:T(8,128)(2,1)S(1)} %get-tuple-element.10), channel_id=1, replica_groups=mesh['replica'=8,'fsdp'=96] {'replica'}, dimensions={0}, use_global_device_ids=true | all-gather | bytes 1032192 | tf_op jit(solution)/shard_map/all_gather | solution.py:407
  60.9 0.0 copy-start.6
  60.9 2.7 %update.1.after_ref = bf16[96,2,384]{2,1,0:T(2,128)(2,1)} custom-call(s32[1,72]{1,0:T(1,128)S(1)} %bitcast.16, s32[1,72]{1,0:T(1,128)S(1)} %bitcast.19, s32[1,72]{1,0:T(1,128)S(1)} %bitcast.21, bf16[512,896]{1,0:T(8,128)(2,1)S(1)} %all_gather.3.block_ref, bf16[768,512]{1,0:T(8,128)(2,1)S(1)} %get-tuple-element.11.right_ref, ...), custom_call_target="tpu_custom_call" | custom-call | flops 1073741824 | bytes 1048576 | tf_op jit(solution)/shard_map/update/pallas_call | solution.py:408
  63.7 0.0 copy-start.5
  63.7 11.0 %all-to-all-start.1 = ((bf16[96,2,384]{2,1,0:T(2,128)(2,1)}), bf16[96,2,384]{2,1,0:T(2,128)(2,1)S(1)}, u32[]{:S(2)}, u32[]{:S(2)}) async-start(bf16[96,2,384]{2,1,0:T(2,128)(2,1)} %update.1.after_ref), calls=%async_computation.1 | async-start | bytes 294912 | tf_op jit(solution)/shard_map/all_to_all | solution.py:359
  74.7 0.0 copy-start
  74.7 0.9 %copy-done = bf16[96,2,384]{2,1,0:T(2,128)(2,1)S(1)} copy-done((bf16[96,2,384]{2,1,0:T(2,128)(2,1)S(1)}, bf16[96,2,384]{2,1,0:T(2,128)(2,1)}, u32[]{:S(2)}) %copy-start) | copy-done | bytes 147480
  75.6 4.4 %stats.1 = (f32[84,672]{1,0:T(8,128)S(1)}, f32[84,672]{1,0:T(8,128)S(1)}) custom-call(bf16[512,896]{1,0:T(8,128)(2,1)S(1)} %all_gather.3.block_ref, bf16[88,672]{1,0:T(8,128)(2,1)S(1)} %get-tuple-element.14.columns_ref, bf16[96,2,384]{2,1,0:T(2,128)(2,1)S(1)} %copy-done), custom_call_target="tpu_custom_call" | custom-call | flops 536870912 | bytes 1048576 | tf_op jit(solution)/shard_map/stats/pallas_call | solution.py:428
  80.0 0.0 copy-done.6
  80.0 0.0 copy-done.5
  80.0 0.1 bitcast_add_fusion
  80.2 1.0 %copy.14 = f32[1,84,672]{2,0,1:T(1,128)} copy(f32[1,84,672]{2,1,0:T(8,128)S(1)} %get-tuple-element.20) | data formatting | bytes 451584
  81.1 1.0 %copy.13 = f32[1,84,672]{2,0,1:T(1,128)} copy(f32[1,84,672]{2,1,0:T(8,128)S(1)} %get-tuple-element.21) | data formatting | bytes 451584
  82.1 7.9 %all-to-all-done.1.wire_ref = bf16[96,2,384]{2,1,0:T(2,128)(2,1)S(1)} async-done(((bf16[96,2,384]{2,1,0:T(2,128)(2,1)}), bf16[96,2,384]{2,1,0:T(2,128)(2,1)S(1)}, u32[]{:S(2)}, u32[]{:S(2)}) %all-to-all-start.1) | async-done | bytes 147488 | tf_op jit(solution)/shard_map/all_to_all | solution.py:359
  90.0 1.0 %unpack.1 = bf16[7,72,84]{2,1,0:T(8,128)(2,1)} custom-call(s32[1,72]{1,0:T(1,128)S(1)} %bitcast.17, bf16[96,2,384]{2,1,0:T(2,128)(2,1)S(1)} %all-to-all-done.1.wire_ref), custom_call_target="tpu_custom_call" | custom-call | flops 1048576 | bytes 1048576 | tf_op jit(solution)/shard_map/unpack/pallas_call | solution.py:438
Async XLA Ops:
  2.6 35.1 %all-to-all-start = ((bf16[96,2,384]{2,1,0:T(2,128)(2,1)}), bf16[96,2,384]{2,1,0:T(2,128)(2,1)S(1)}, u32[]{:S(2)}, u32[]{:S(2)}) async-start(bf16[96,2,384]{2,1,0:T(2,128)(2,1)} %pack.1), calls=%async_computation | async-start | bytes 294912 | tf_op jit(solution)/shard_map/all_to_all | solution.py:359
  23.6 1.6 %copy-start.4 = (f32[1,672,672]{2,1,0:T(8,128)S(1)}, f32[1,672,672]{2,1,0:T(8,128)}, u32[]{:S(2)}) copy-start(f32[1,672,672]{2,1,0:T(8,128)} %param.14) | copy-start | bytes 5419012
  25.2 12.5 %copy-start.1 = (s32[72]{0:T(128)S(1)}, s32[72]{0:T(128)}, u32[]{:S(2)}) copy-start(s32[72]{0:T(128)} %param.9) | copy-start | bytes 868
  25.2 12.5 %copy-start.2 = (s32[72]{0:T(128)S(1)}, s32[72]{0:T(128)}, u32[]{:S(2)}) copy-start(s32[72]{0:T(128)} %param.10) | copy-start | bytes 868
  25.2 12.5 %copy-start.3 = (s32[72]{0:T(128)S(1)}, s32[72]{0:T(128)}, u32[]{:S(2)}) copy-start(s32[72]{0:T(128)} %param.11) | copy-start | bytes 868
  60.9 19.1 %copy-start.6 = (f32[1,84,672]{2,0,1:T(1,128)S(1)}, f32[1,84,672]{2,0,1:T(1,128)}, u32[]{:S(2)}) copy-start(f32[1,84,672]{2,0,1:T(1,128)} %param.12) | copy-start | bytes 677380
  63.7 16.3 %copy-start.5 = (f32[1,84,672]{2,0,1:T(1,128)S(1)}, f32[1,84,672]{2,0,1:T(1,128)}, u32[]{:S(2)}) copy-start(f32[1,84,672]{2,0,1:T(1,128)} %param.13) | copy-start | bytes 677380
  63.7 26.3 %all-to-all-start.1 = ((bf16[96,2,384]{2,1,0:T(2,128)(2,1)}), bf16[96,2,384]{2,1,0:T(2,128)(2,1)S(1)}, u32[]{:S(2)}, u32[]{:S(2)}) async-start(bf16[96,2,384]{2,1,0:T(2,128)(2,1)} %update.1.after_ref), calls=%async_computation.1 | async-start | bytes 294912 | tf_op jit(solution)/shard_map/all_to_all | solution.py:359
  74.7 0.9 %copy-start = (bf16[96,2,384]{2,1,0:T(2,128)(2,1)S(1)}, bf16[96,2,384]{2,1,0:T(2,128)(2,1)}, u32[]{:S(2)}) copy-start(bf16[96,2,384]{2,1,0:T(2,128)(2,1)} %update.1.after_ref) | copy-start | bytes 442372
